TPU v7x, 128 devices: a whole 4x4x4 slice. The times are simulated.
128 devices in a mesh: dp: 16 (over x, y), row: 2 (over z_lo), col: 4 (over z_hi, core).
Axes of the slice: x: 4, y: 4, z: 4 (z_hi: 2, z_lo: 2; z = z_hi * 2 + z_lo), core: 2. Of those that a mesh axis runs over, the one named last changes fastest.
Arguments:
- tokens: bfloat16 [16384, 1152], P(('dp', 'col'), 'row'), may hold values from -6 to 6
- doc_lengths: int32 [16, 6], P('dp'), may hold values from 0 to 1024, as said below
- w_query: bfloat16 [1152, 1024], P('row', 'col'), may hold values from -0.1875 to 0.1875
- w_key: bfloat16 [1152, 256], P('row', 'col'), may hold values from -0.1875 to 0.1875
- w_value: bfloat16 [1152, 256], P('row', 'col'), may hold values from -0.1875 to 0.1875
- w_out: bfloat16 [1024, 1152], P('col', 'row'), may hold values from -0.1875 to 0.1875
- w_gate: bfloat16 [1152, 6912], P('row', 'col'), may hold values from -0.1875 to 0.1875
- w_up: bfloat16 [1152, 6912], P('row', 'col'), may hold values from -0.1875 to 0.1875
- w_down: bfloat16 [6912, 1152], P('col', 'row'), may hold values from -0.078125 to 0.078125
- gain_attn_in: float32 [1152], P('row'), may hold values from 0.25 to 1.75
- gain_attn_out: float32 [1152], P('row'), may hold values from 0.25 to 1.75
- gain_ff_in: float32 [1152], P('row'), may hold values from 0.25 to 1.75
- gain_ff_out: float32 [1152], P('row'), may hold values from 0.25 to 1.75
- gain_query: float32 [256], replicated, may hold values from 0.25 to 1.75
- gain_key: float32 [256], replicated, may hold values from 0.25 to 1.75
- cotangent: bfloat16 [16384, 1152], P(('dp', 'col'), 'row'), may hold values from -6 to 6
Outputs:
- mixed: bfloat16 [16384, 1152], P(('dp', 'col'), 'row')
- grad_tokens: float32 [16384, 1152], P(('dp', 'col'), 'row')
- grad_w_query: float32 [1152, 1024], P('row', 'col')
- grad_w_key: float32 [1152, 256], P('row', 'col')
- grad_w_value: float32 [1152, 256], P('row', 'col')
- grad_w_out: float32 [1024, 1152], P('col', 'row')
- grad_w_gate: float32 [1152, 6912], P('row', 'col')
- grad_w_up: float32 [1152, 6912], P('row', 'col')
- grad_w_down: float32 [6912, 1152], P('col', 'row')
- grad_gain_attn_in: float32 [1152], P('row')
- grad_gain_attn_out: float32 [1152], P('row')
- grad_gain_ff_in: float32 [1152], P('row')
- grad_gain_ff_out: float32 [1152], P('row')
- grad_gain_query: float32 [256], replicated
- grad_gain_key: float32 [256], replicated
Inputs may be any that keep to these rules, and one draw needn't show every extreme that they name: `doc_lengths`: row g lists the lengths of data group g's sequences in the order in which they lie in its 1024 slots; zeros are empty entries. Each row sums to at most 1024; in every draw one row is a single sequence of exactly 1024. In every row one sequence begins in the first 256 slots and ends in the last 256.
All inputs are finite; a program needn't handle non-finite values.
Results may differ from a plain program's by a relative error of at most 0.025.
Values may be sent and summed in bfloat16 or wider, within the bound.
No kernel may reach another device: no remote copies, remote signals or barrier semaphores. Data moves between devices by JAX's collectives and lax.ppermute only.
A program may use at most 128 MiB of HBM per device.

v0:
```python
import jax
import jax.numpy as jnp
from jax import lax
from jax.sharding import PartitionSpec as P

WINDOW = 512


EPSILON = 1e-06
ROPE_BASE = 10000.0
MASKED = -1e30


def layout(lengths_row, capacity):
    slot_count = lengths_row.shape[0]
    seq_ends = jnp.cumsum(lengths_row)
    places = jnp.arange(capacity, dtype=jnp.int32)
    sequence = jnp.sum((places[:, None] >= seq_ends[None, :]).astype(jnp.int32), axis=1)
    starts = jnp.concatenate([jnp.zeros((1,), jnp.int32), seq_ends])
    labels = jnp.arange(slot_count + 1, dtype=jnp.int32)
    start_of = jnp.sum(jnp.where(sequence[:, None] == labels[None, :], starts[None, :], 0), axis=1)
    live_rows = (places < seq_ends[slot_count - 1]).astype(jnp.int32)
    return (sequence, places - start_of, live_rows)


def norm_rows(values, gain_vector):
    return (
        values
        * lax.rsqrt(jnp.mean(values * values, axis=-1, keepdims=True) + EPSILON)
        * gain_vector
    )


def rotate(values, positions):
    full_width = values.shape[-1]
    half_width = full_width // 2
    frequency = ROPE_BASE ** (-2.0 * jnp.arange(half_width, dtype=jnp.float32) / full_width)
    angles = positions.astype(jnp.float32).reshape((-1,) + (1,) * (values.ndim - 1)) * frequency
    cosine = jnp.cos(angles)
    sine_part = jnp.sin(angles)
    first_half = values[..., :half_width]
    second_half = values[..., half_width:]
    return jnp.concatenate(
        [
            first_half * cosine - second_half * sine_part,
            second_half * cosine + first_half * sine_part,
        ],
        axis=-1,
    )


def normed_rotated(raw_values, gain_vector, positions):
    return rotate(norm_rows(raw_values, gain_vector), positions)


def row_total(values):
    return lax.psum(values, "row")


def norm_forward(values, gain_vector, full_width):
    inverse = lax.rsqrt(row_total(jnp.sum(values * values, axis=1)) / full_width + EPSILON)
    return (values * inverse[:, None] * gain_vector[None, :], inverse)


def norm_backward(values, inverse, gain_vector, incoming, full_width):
    gain_grad = jnp.sum(incoming * values * inverse[:, None], axis=0)
    inner_sum = row_total(jnp.sum(incoming * gain_vector[None, :] * values, axis=1))
    cubed_term = inverse * inverse * inverse * inner_sum / full_width
    return (
        inverse[:, None] * gain_vector[None, :] * incoming - values * cubed_term[:, None],
        gain_grad,
    )


def times_transposed(left, right):
    return lax.dot_general(
        left, right, (((1,), (1,)), ((), ())), preferred_element_type=jnp.float32
    )


def contract_rows(left, right):
    return lax.dot_general(
        left, right, (((0,), (0,)), ((), ())), preferred_element_type=jnp.float32
    )


def spread_cols(low_rows):
    return lax.all_gather(low_rows, "col", axis=0, tiled=True)


def lift_rows(low_rows, transform):
    gathered = spread_cols(low_rows)
    return (lax.psum_scatter(transform(gathered), "row", scatter_dimension=0, tiled=True), gathered)


def sink_rows(low_rows, transform):
    gathered = lax.all_gather(low_rows, "row", axis=0, tiled=True)
    return (
        lax.psum_scatter(
            transform(gathered).astype(jnp.bfloat16), "col", scatter_dimension=0, tiled=True
        ).astype(jnp.float32),
        gathered,
    )


def assemble(gathered, size_row, size_col):
    half_rows = gathered.shape[1]
    part_width = gathered.shape[2] // 2
    arranged = gathered.reshape(size_row, size_col, half_rows, 2, part_width).transpose(
        0, 2, 3, 1, 4
    )
    arranged = arranged.reshape(size_row * half_rows, 2, size_col * part_width)
    return (arranged[:, 0], arranged[:, 1])


def disassemble(grad_keys, grad_values, size_row, size_col):
    capacity = grad_keys.shape[0]
    head_dim = grad_keys.shape[1]
    stacked = jnp.stack([grad_keys, grad_values], axis=1)
    arranged = stacked.reshape(
        size_row, capacity // size_row, 2, size_col, head_dim // size_col
    ).transpose(0, 3, 1, 2, 4)
    return arranged.reshape(size_row * size_col, capacity // size_row, 2 * head_dim // size_col)


def block_context(keys_low, values_low, sequence, positions, row_seq, row_pos):
    distance = row_pos[:, None] - positions[None, :]
    allowed = (row_seq[:, None] == sequence[None, :]) & (distance >= 0) & (distance < WINDOW)
    return (keys_low, values_low, allowed)


def masked_scores(query_part, key_part, allowed, score_scale):
    raw_scores = jnp.einsum("qhd,kd->hqk", query_part, key_part, preferred_element_type=jnp.float32)
    return jnp.where(allowed[None], raw_scores * score_scale, MASKED)


def body(
    tokens,
    doc_lengths,
    w_query,
    w_key,
    w_value,
    w_out,
    w_gate,
    w_up,
    w_down,
    gain_attn_in,
    gain_attn_out,
    gain_ff_in,
    gain_ff_out,
    gain_query,
    gain_key,
    cotangent,
):
    size_row = lax.axis_size("row")
    size_col = lax.axis_size("col")
    own_rows = tokens.shape[0]
    capacity = own_rows * size_col
    half_rows = capacity // size_row
    part_width = tokens.shape[1]
    full_width = part_width * size_row
    head_dim = gain_query.shape[0]
    local_heads = w_query.shape[1] // head_dim
    query_width = local_heads * head_dim
    key_width = w_key.shape[1]
    hidden_width = w_gate.shape[1]
    score_scale = head_dim ** (-0.5)
    sequence, positions, live_rows = layout(doc_lengths[0], capacity)
    own_first = lax.axis_index("col") * own_rows
    half_first = lax.axis_index("row") * half_rows
    live_own = lax.dynamic_slice_in_dim(live_rows, own_first, own_rows, 0).astype(jnp.float32)
    query_seq = lax.dynamic_slice_in_dim(sequence, half_first, half_rows, 0)
    query_pos = lax.dynamic_slice_in_dim(positions, half_first, half_rows, 0)
    residual = tokens.astype(jnp.float32)
    normed_in, inverse_in = norm_forward(residual, gain_attn_in, full_width)
    normed_low = normed_in.astype(jnp.bfloat16)
    weights_qkv = jnp.concatenate([w_query, w_key, w_value], axis=1)
    projected, gathered_in = lift_rows(
        normed_low, lambda pieces: jnp.dot(pieces, weights_qkv, preferred_element_type=jnp.float32)
    )
    pre_query = projected[:, :query_width].reshape(half_rows, local_heads, head_dim)
    key_value_piece = projected[:, query_width:].astype(jnp.bfloat16)
    gathered_kv = lax.all_gather(key_value_piece[None], ("row", "col"), axis=0, tiled=True)
    keys_pre, values_low = assemble(gathered_kv, size_row, size_col)
    queries, query_back = jax.vjp(
        lambda raw_values, gain_vector: normed_rotated(raw_values, gain_vector, query_pos),
        pre_query,
        gain_query,
    )
    keys_turned, key_back = jax.vjp(
        lambda raw_values, gain_vector: normed_rotated(raw_values, gain_vector, positions),
        keys_pre.astype(jnp.float32),
        gain_key,
    )
    queries_low = queries.astype(jnp.bfloat16)
    keys_low = keys_turned.astype(jnp.bfloat16)
    key_part, value_part, allowed = block_context(
        keys_low, values_low, sequence, positions, query_seq, query_pos
    )
    scores = masked_scores(queries_low, key_part, allowed, score_scale)
    highest = jnp.max(scores, axis=2, keepdims=True)
    weights = jnp.exp(scores - highest)
    totals = jnp.sum(weights, axis=2, keepdims=True)
    shares_low = (weights / totals).astype(jnp.bfloat16)
    attended_parts = jnp.einsum(
        "hqk,kd->qhd", shares_low, value_part, preferred_element_type=jnp.float32
    ).astype(jnp.bfloat16)
    log_totals = highest + jnp.log(totals)
    attended = attended_parts.reshape(half_rows, query_width)
    branch_attn, gathered_attn = sink_rows(
        attended, lambda pieces: jnp.dot(pieces, w_out, preferred_element_type=jnp.float32)
    )
    normed_attn_out, inverse_attn_out = norm_forward(branch_attn, gain_attn_out, full_width)
    hidden_mid = residual + normed_attn_out
    normed_ff, inverse_ff_in = norm_forward(hidden_mid, gain_ff_in, full_width)
    normed_ff_low = normed_ff.astype(jnp.bfloat16)
    weights_both = jnp.concatenate([w_gate, w_up], axis=1)
    gate_up, gathered_ff = lift_rows(
        normed_ff_low,
        lambda pieces: jnp.dot(pieces, weights_both, preferred_element_type=jnp.float32),
    )
    activated, activate_back = jax.vjp(
        lambda gate_part, upward_part: jax.nn.gelu(gate_part, approximate=True) * upward_part,
        gate_up[:, :hidden_width],
        gate_up[:, hidden_width:],
    )
    activated_low = activated.astype(jnp.bfloat16)
    branch_ff, gathered_hidden = sink_rows(
        activated_low, lambda pieces: jnp.dot(pieces, w_down, preferred_element_type=jnp.float32)
    )
    normed_ff_out, inverse_ff_out = norm_forward(branch_ff, gain_ff_out, full_width)
    mixed = (hidden_mid + normed_ff_out).astype(jnp.bfloat16)
    grad_result = cotangent.astype(jnp.float32) * live_own[:, None]
    grad_branch_ff, grad_gain_ff_out = norm_backward(
        branch_ff, inverse_ff_out, gain_ff_out, grad_result, full_width
    )
    grad_activated, gathered_grad_ff = lift_rows(
        grad_branch_ff.astype(jnp.bfloat16), lambda pieces: times_transposed(pieces, w_down)
    )
    grad_w_down = contract_rows(gathered_hidden, gathered_grad_ff)
    grad_gate, grad_up = activate_back(grad_activated)
    grad_gate_up = jnp.concatenate([grad_gate, grad_up], axis=1).astype(jnp.bfloat16)
    grad_normed_ff, gathered_grad_gu = sink_rows(
        grad_gate_up, lambda pieces: times_transposed(pieces, weights_both)
    )
    grad_both = contract_rows(gathered_ff, gathered_grad_gu)
    grad_hidden, grad_gain_ff_in = norm_backward(
        hidden_mid, inverse_ff_in, gain_ff_in, grad_normed_ff, full_width
    )
    grad_hidden = grad_hidden + grad_result
    grad_branch_attn, grad_gain_attn_out = norm_backward(
        branch_attn, inverse_attn_out, gain_attn_out, grad_hidden, full_width
    )
    grad_attended, gathered_grad_attn = lift_rows(
        grad_branch_attn.astype(jnp.bfloat16), lambda pieces: times_transposed(pieces, w_out)
    )
    grad_w_out = contract_rows(gathered_attn, gathered_grad_attn)
    grad_out_low = grad_attended.astype(jnp.bfloat16).reshape(half_rows, local_heads, head_dim)
    key_part, value_part, allowed = block_context(
        keys_low, values_low, sequence, positions, query_seq, query_pos
    )
    scores = masked_scores(queries_low, key_part, allowed, score_scale)
    shares = jnp.exp(scores - log_totals)
    grad_shares = jnp.einsum(
        "qhd,kd->hqk", grad_out_low, value_part, preferred_element_type=jnp.float32
    )
    inner_sum = jnp.sum(shares * grad_shares, axis=2, keepdims=True)
    grad_scores = (shares * (grad_shares - inner_sum) * score_scale).astype(jnp.bfloat16)
    grad_query_parts = jnp.einsum(
        "hqk,kd->qhd", grad_scores, key_part, preferred_element_type=jnp.float32
    )
    grad_keys = jnp.einsum(
        "hqk,qhd->kd", grad_scores, queries_low, preferred_element_type=jnp.float32
    )
    grad_values = jnp.einsum(
        "hqk,qhd->kd", shares.astype(jnp.bfloat16), grad_out_low, preferred_element_type=jnp.float32
    )
    grad_pre_query, grad_gain_query = query_back(grad_query_parts)
    grad_keys_pre, grad_gain_key = key_back(grad_keys)
    grad_kv_piece = lax.psum_scatter(
        disassemble(grad_keys_pre, grad_values, size_row, size_col).astype(jnp.bfloat16),
        ("row", "col"),
        scatter_dimension=0,
        tiled=True,
    ).astype(jnp.float32)[0]
    grad_projected = jnp.concatenate(
        [grad_pre_query.reshape(half_rows, query_width), grad_kv_piece], axis=1
    ).astype(jnp.bfloat16)
    grad_normed_in, gathered_grad_qkv = sink_rows(
        grad_projected, lambda pieces: times_transposed(pieces, weights_qkv)
    )
    grad_weights_qkv = contract_rows(gathered_in, gathered_grad_qkv)
    grad_input, grad_gain_attn_in = norm_backward(
        residual, inverse_in, gain_attn_in, grad_normed_in, full_width
    )
    grad_tokens = grad_hidden + grad_input
    grad_w_query = grad_weights_qkv[:, :query_width]
    grad_w_key = grad_weights_qkv[:, query_width : query_width + key_width]
    grad_w_value = grad_weights_qkv[:, query_width + key_width :]
    grad_w_gate = grad_both[:, :hidden_width]
    grad_w_up = grad_both[:, hidden_width:]
    grad_w_query, grad_w_key, grad_w_value, grad_w_out, grad_w_gate, grad_w_up, grad_w_down = (
        lax.psum(grad_w_query.astype(jnp.bfloat16), "dp").astype(jnp.float32),
        lax.psum(grad_w_key.astype(jnp.bfloat16), "dp").astype(jnp.float32),
        lax.psum(grad_w_value.astype(jnp.bfloat16), "dp").astype(jnp.float32),
        lax.psum(grad_w_out.astype(jnp.bfloat16), "dp").astype(jnp.float32),
        lax.psum(grad_w_gate.astype(jnp.bfloat16), "dp").astype(jnp.float32),
        lax.psum(grad_w_up.astype(jnp.bfloat16), "dp").astype(jnp.float32),
        lax.psum(grad_w_down.astype(jnp.bfloat16), "dp").astype(jnp.float32),
    )
    row_first = lax.axis_index("row") * part_width

    def placed(part_grad):
        return lax.dynamic_update_slice_in_dim(
            jnp.zeros((full_width,), jnp.float32), part_grad, row_first, 0
        )

    summed = lax.psum(
        (
            placed(grad_gain_attn_in),
            placed(grad_gain_attn_out),
            placed(grad_gain_ff_in),
            placed(grad_gain_ff_out),
            grad_gain_query,
            grad_gain_key,
        ),
        ("dp", "row", "col"),
    )

    def own_part(full_grad):
        return lax.dynamic_slice_in_dim(full_grad, row_first, part_width, 0)

    return (
        mixed,
        grad_tokens,
        grad_w_query,
        grad_w_key,
        grad_w_value,
        grad_w_out,
        grad_w_gate,
        grad_w_up,
        grad_w_down,
        own_part(summed[0]),
        own_part(summed[1]),
        own_part(summed[2]),
        own_part(summed[3]),
        summed[4],
        summed[5],
    )


def solution(mesh):
    return jax.shard_map(
        body,
        mesh=mesh,
        in_specs=(
            P(("dp", "col"), "row"),
            P("dp", None),
            P("row", "col"),
            P("row", "col"),
            P("row", "col"),
            P("col", "row"),
            P("row", "col"),
            P("row", "col"),
            P("col", "row"),
            P("row"),
            P("row"),
            P("row"),
            P("row"),
            P(),
            P(),
            P(("dp", "col"), "row"),
        ),
        out_specs=(
            P(("dp", "col"), "row"),
            P(("dp", "col"), "row"),
            P("row", "col"),
            P("row", "col"),
            P("row", "col"),
            P("col", "row"),
            P("row", "col"),
            P("row", "col"),
            P("col", "row"),
            P("row"),
            P("row"),
            P("row"),
            P("row"),
            P(),
            P(),
        ),
        check_vma=False,
    )
```

profile of v0, /device:TPU:1, one launch (start us, length us, event | category | flops | bytes accessed | tf_op | source)
XLA Modules:
  0.0 1086.2 jit_solution(17616424376334829351)
XLA Ops:
  8.4 4.8 psum.147
  13.2 1.8 fusion.62
  17.3 23.5 %all-gather.10.cloned.1.call-done = bf16[1024,576]{0,1:T(8,128)(2,1)} async-done(((bf16[256,576]{0,1:T(8,128)(2,1)}), bf16[1024,576]{0,1:T(8,128)(2,1)}) %all-gather.10.cloned.1.call-update) | async-done | bytes 1179664 | tf_op jit(solution)/shard_map/all_gather | solution.py:88
  40.8 3.5 fusion.97
  44.4 27.6 %reduce-scatter.10.cloned.1.call-done = f32[512,384]{1,0:T(8,128)} async-done(((f32[1024,384]{1,0:T(8,128)}), f32[512,384]{1,0:T(8,128)}) %reduce-scatter.10.cloned.1.call-update) | async-done | bytes 786448 | tf_op jit(solution)/shard_map/reduce_scatter | solution.py:93
  78.2 30.9 %all-gather.22.cloned.1.call-done = bf16[4096,128]{1,0:T(8,128)(2,1)} async-done(((bf16[512,128]{1,0:T(8,128)(2,1)}), bf16[4096,128]{1,0:T(8,128)(2,1)}) %all-gather.22.cloned.1.call-update) | async-done | bytes 1048592 | tf_op jit(solution)/shard_map/all_gather | solution.py:183
  112.1 3.0 copy.58
  115.1 1.8 reshape.428
  120.5 2.4 fusion.67
  126.3 8.4 all-gather.1
  136.4 32.0 %reduce-scatter.12.cloned.1.call-done = bf16[256,576]{0,1:T(8,128)(2,1)} async-done(((bf16[1024,576]{0,1:T(8,128)(2,1)}), bf16[256,576]{0,1:T(8,128)(2,1)}) %reduce-scatter.12.cloned.1.call-update) | async-done | bytes 294928 | tf_op jit(solution)/shard_map/reduce_scatter | solution.py:99
  169.4 4.3 psum.148
  174.4 1.7 multiply_reduce_fusion
  176.1 4.5 psum.149
  181.9 1.9 multiply_convert_fusion.2
  184.0 23.6 %all-gather.12.cloned.1.call-done = bf16[1024,576]{0,1:T(8,128)(2,1)} async-done(((bf16[256,576]{0,1:T(8,128)(2,1)}), bf16[1024,576]{0,1:T(8,128)(2,1)}) %all-gather.12.cloned.1.call-update) | async-done | bytes 1179664 | tf_op jit(solution)/shard_map/all_gather | solution.py:88
  207.7 11.6 %fusion.8 = f32[1024,3456]{1,0:T(8,128)} fusion(bf16[1024,576]{0,1:T(8,128)(2,1)} %all-gather.12.cloned.1.call-done, bf16[576,1728]{1,0:T(8,128)(2,1)} %param.23, bf16[576,1728]{1,0:T(8,128)(2,1)} %param.22), kind=kOutput, calls=%fused_computation.19 | convolution fusion | flops 4084826112 | bytes 19316736 | tf_op jit(solution)/shard_map/dot_general | solution.py:220
  219.4 162.9 %reduce-scatter.14.cloned.1.call-done = f32[512,3456]{1,0:T(8,128)} async-done(((f32[1024,3456]{1,0:T(8,128)}), f32[512,3456]{1,0:T(8,128)}) %reduce-scatter.14.cloned.1.call-update) | async-done | bytes 7077904 | tf_op jit(solution)/shard_map/reduce_scatter | solution.py:93
  382.3 5.8 multiply_convert_fusion.1
  388.2 54.5 %all-gather.14.cloned.1.call-done = bf16[1024,1728]{1,0:T(8,128)(2,1)} async-done(((bf16[512,1728]{1,0:T(8,128)(2,1)}), bf16[1024,1728]{1,0:T(8,128)(2,1)}) %all-gather.14.cloned.1.call-update) | async-done | bytes 3538960 | tf_op jit(solution)/shard_map/all_gather | solution.py:97
  442.7 5.4 convolution_convert_fusion.4
  450.7 31.3 %reduce-scatter.16.cloned.1.call-done = bf16[256,576]{0,1:T(8,128)(2,1)} async-done(((bf16[1024,576]{0,1:T(8,128)(2,1)}), bf16[256,576]{0,1:T(8,128)(2,1)}) %reduce-scatter.16.cloned.1.call-update) | async-done | bytes 294928 | tf_op jit(solution)/shard_map/reduce_scatter | solution.py:99
  482.0 1.6 fusion.51
  483.6 4.5 psum.150
  489.3 2.0 fusion.59
  491.3 4.5 psum.151
  496.4 1.9 fusion.57
  498.4 23.8 %all-gather.16.cloned.1.call-done = bf16[1024,576]{0,1:T(8,128)(2,1)} async-done(((bf16[256,576]{0,1:T(8,128)(2,1)}), bf16[1024,576]{0,1:T(8,128)(2,1)}) %all-gather.16.cloned.1.call-update) | async-done | bytes 1179664 | tf_op jit(solution)/shard_map/all_gather | solution.py:88
  522.2 6.7 fusion.122
  529.0 89.9 %reduce-scatter.18.cloned.1.call-done = f32[512,1728]{1,0:T(8,128)} async-done(((f32[1024,1728]{1,0:T(8,128)}), f32[512,1728]{1,0:T(8,128)}) %reduce-scatter.18.cloned.1.call-update) | async-done | bytes 3538960 | tf_op jit(solution)/shard_map/reduce_scatter | solution.py:93
  618.9 5.8 fusion.6
  624.7 2.7 pad_maximum_fusion.1
  628.0 92.4 %all-gather.18.cloned.1.call-done = bf16[1024,3456]{1,0:T(8,128)(2,1)} async-done(((bf16[512,3456]{1,0:T(8,128)(2,1)}), bf16[1024,3456]{1,0:T(8,128)(2,1)}) %all-gather.18.cloned.1.call-update) | async-done | bytes 7077904 | tf_op jit(solution)/shard_map/all_gather | solution.py:97
  720.4 9.6 fusion.17
  730.1 33.9 %reduce-scatter.20.cloned.1.call-done = bf16[256,576]{0,1:T(8,128)(2,1)} async-done(((bf16[1024,576]{0,1:T(8,128)(2,1)}), bf16[256,576]{0,1:T(8,128)(2,1)}) %reduce-scatter.20.cloned.1.call-update) | async-done | bytes 294928 | tf_op jit(solution)/shard_map/reduce_scatter | solution.py:99
  765.4 3.9 psum.152
  769.4 2.8 fusion.50
  772.2 3.8 psum.153
  776.9 23.8 %all-gather.20.cloned.1.call-done = bf16[1024,576]{0,1:T(8,128)(2,1)} async-done(((bf16[256,576]{0,1:T(8,128)(2,1)}), bf16[1024,576]{0,1:T(8,128)(2,1)}) %all-gather.20.cloned.1.call-update) | async-done | bytes 1179664 | tf_op jit(solution)/shard_map/all_gather | solution.py:88
  800.7 2.9 fusion.123
  803.6 21.8 %reduce-scatter.22.cloned.1.call-done = f32[512,256]{1,0:T(8,128)} async-done(((f32[1024,256]{1,0:T(8,128)}), f32[512,256]{1,0:T(8,128)}) %reduce-scatter.22.cloned.1.call-update) | async-done | bytes 524304 | tf_op jit(solution)/shard_map/reduce_scatter | solution.py:93
  826.6 2.6 fusion.9
  831.6 2.3 fusion.70
  835.5 2.8 reshape.443
  839.9 1.7 fusion.20
  842.8 2.3 copy.66
  845.3 6.1 convolution_convert_fusion.1
  853.7 26.4 %reduce-scatter.24.cloned.1.call-done = bf16[1,512,128]{2,1,0:T(8,128)(2,1)} async-done(((bf16[8,512,128]{2,1,0:T(8,128)(2,1)}), bf16[1,512,128]{2,1,0:T(8,128)(2,1)}) %reduce-scatter.24.cloned.1.call-update) | async-done | bytes 131088 | tf_op jit(solution)/shard_map/reduce_scatter | solution.py:280
  881.1 10.6 all_gather.35
  891.7 2.8 convolution_convert_fusion.3
  894.6 7.8 convolution_convert_fusion
  902.4 3.0 fusion.119
  910.4 17.2 %reduce-scatter.26.cloned.1.call-done = bf16[256,576]{0,1:T(8,128)(2,1)} async-done(((bf16[1024,576]{0,1:T(8,128)(2,1)}), bf16[256,576]{0,1:T(8,128)(2,1)}) %reduce-scatter.26.cloned.1.call-update) | async-done | bytes 294928 | tf_op jit(solution)/shard_map/reduce_scatter | solution.py:99
  929.2 67.4 %all-reduce.4 = (f32[1152]{0:T(1024)S(1)}, f32[1152]{0:T(1024)S(1)}, f32[1152]{0:T(1024)S(1)}, f32[1152]{0:T(1024)S(1)}, f32[256]{0:T(256)}, /*index=5*/f32[256]{0:T(256)}) all-reduce(f32[1152]{0:T(1024)S(1)} %dynamic_update_slice.12, ...), channel_id=1, replica_groups=mesh['dp'=16,'row'=2,'col'=4] {'dp','row','col'}, use_global_device_ids=true, to_apply=%region_43.44 | all-reduce | flops 5120 | bytes 40960 | tf_op jit(solution)/shard_map/psum | solution.py:318
  999.3 3.8 psum.154
  1003.1 2.0 fusion.43
  1005.1 58.8 %all-reduce.8.cloned.1.call-done = (bf16[576,64]{1,0:T(8,128)(2,1)}, bf16[576,64]{1,0:T(8,128)(2,1)}, bf16[576,256]{1,0:T(8,128)(2,1)}, bf16[256,576]{0,1:T(8,12...) async-done(((bf16[576,64]{1,0:T(8,128)(2,1)}, bf16[576,64]{1,0:T(8,128)(2,1)}, bf16[576,256]{1,0:T(8,128)(2,1)}, ...) | async-done | bytes 6709264 | tf_op jit(solution)/shard_map/psum | solution.py:304
  1063.9 1.7 copy.67
  1065.6 1.7 copy.68
  1067.2 1.8 convert_element_type.175
  1069.1 1.8 convert_element_type.179
  1070.9 4.0 convert_element_type.180
  1074.9 2.3 convert_element_type.181
  1077.2 2.3 convert_element_type.183
  (249 shorter events, 52.8 us)
Async XLA Ops:
  7.2 435.5 %copy-start = (bf16[1728,576]{0,1:T(8,128)(2,1)S(1)}, bf16[1728,576]{0,1:T(8,128)(2,1)}, u32[]{:S(2)}) copy-start(bf16[1728,576]{0,1:T(8,128)(2,1)} %param.24) | copy-start | bytes 5971972
  7.2 33.6 %all-gather.10.cloned.1.call-start = ((), (), s32[]{:S(2)}) async-start(), calls=%async_computation.9 | async-start | bytes 1474560 | tf_op jit(solution)/shard_map/all_gather | solution.py:88
  15.1 56.8 %reduce-scatter.10.cloned.1.call-start = ((), (), s32[]{:S(2)}) async-start(), calls=%async_computation.10 | async-start | bytes 2359296 | tf_op jit(solution)/shard_map/reduce_scatter | solution.py:93
  16.2 28.1 %copy-start.24 = (bf16[576,64]{1,0:T(8,128)(2,1)}, bf16[576,64]{1,0:T(8,128)(2,1)S(1)}, u32[]{:S(2)}) copy-start(bf16[576,64]{1,0:T(8,128)(2,1)S(1)} %copy.55) | copy-start | bytes 221188
  17.3 27.0 %copy-start.26 = (bf16[576,64]{1,0:T(8,128)(2,1)}, bf16[576,64]{1,0:T(8,128)(2,1)S(1)}, u32[]{:S(2)}) copy-start(bf16[576,64]{1,0:T(8,128)(2,1)S(1)} %copy.56) | copy-start | bytes 221188
  17.3 56.4 %copy-start.69 = (s32[1,6]{1,0:T(1,128)S(1)}, s32[1,6]{1,0:T(1,128)}, u32[]{:S(2)}) copy-start(s32[1,6]{1,0:T(1,128)} %param.17) | copy-start | bytes 76
  44.3 31.5 %copy-start.59 = (f32[256]{0:T(256)S(1)}, f32[256]{0:T(256)}, u32[]{:S(2)}) copy-start(f32[256]{0:T(256)} %param.29) | copy-start | bytes 3076
  44.3 64.7 %all-gather.22.cloned.1.call-start = ((), (), s32[]{:S(2)}) async-start(), calls=%async_computation.24 | async-start | bytes 1179648 | tf_op jit(solution)/shard_map/all_gather | solution.py:183
  73.6 94.7 %reduce-scatter.12.cloned.1.call-start = ((), (), s32[]{:S(2)}) async-start(), calls=%async_computation.11 | async-start | bytes 1474560 | tf_op jit(solution)/shard_map/reduce_scatter | solution.py:99
  74.0 46.4 %copy-start.61 = (f32[128]{0:T(128)}, f32[128]{0:T(128)S(1)}, u32[]{:S(2)}) copy-start(f32[128]{0:T(128)S(1)} %multiply_power_fusion) | copy-start | bytes 1540
  74.4 46.0 %copy-start.32 = (f32[1024]{0:T(1024)}, f32[1024]{0:T(1024)S(1)}, u32[]{:S(2)}) copy-start(f32[1024]{0:T(1024)S(1)} %get-tuple-element.105) | copy-start | bytes 12292
  74.5 36.0 %copy-start.40 = (f32[512]{0:T(512)}, f32[512]{0:T(512)S(1)}, u32[]{:S(2)}) copy-start(f32[512]{0:T(512)S(1)} %get-tuple-element.86) | copy-start | bytes 6148
  78.2 44.7 %copy-start.16 = (bf16[512,128]{1,0:T(8,128)(2,1)}, bf16[512,128]{1,0:T(8,128)(2,1)S(1)}, u32[]{:S(2)}) copy-start(bf16[512,128]{1,0:T(8,128)(2,1)S(1)} %get-tuple-element.102) | copy-start | bytes 393220
  115.1 5.1 copy-start.57
  120.2 3.5 copy-start.34
  123.7 2.6 copy-start.2
  125.7 9.0 copy-start.18
  126.3 48.1 %copy-start.4 = (bf16[256,576]{0,1:T(8,128)(2,1)S(1)}, bf16[256,576]{0,1:T(8,128)(2,1)}, u32[]{:S(2)}) copy-start(bf16[256,576]{0,1:T(8,128)(2,1)} %param.16) | copy-start | bytes 884740
  126.3 48.1 %copy-start.28 = (f32[576]{0:T(1024)S(1)}, f32[576]{0:T(1024)}, u32[]{:S(2)}) copy-start(f32[576]{0:T(1024)} %param.26) | copy-start | bytes 6916
  134.8 47.1 %copy-start.29 = (f32[576]{0:T(1024)S(1)}, f32[576]{0:T(1024)}, u32[]{:S(2)}) copy-start(f32[576]{0:T(1024)} %param.27) | copy-start | bytes 6916
  136.3 71.4 %all-gather.12.cloned.1.call-start = ((), (), s32[]{:S(2)}) async-start(), calls=%async_computation.12 | async-start | bytes 1474560 | tf_op jit(solution)/shard_map/all_gather | solution.py:88
  174.4 44.9 %copy-start.36 = (f32[256]{0:T(256)}, f32[256]{0:T(256)S(1)}, u32[]{:S(2)}) copy-start(f32[256]{0:T(256)S(1)} %add_rsqrt_fusion.2) | copy-start | bytes 3076
  183.8 198.5 %reduce-scatter.14.cloned.1.call-start = ((), (), s32[]{:S(2)}) async-start(), calls=%async_computation.13 | async-start | bytes 21233664 | tf_op jit(solution)/shard_map/reduce_scatter | solution.py:93
  219.3 223.3 %all-gather.14.cloned.1.call-start = ((), (), s32[]{:S(2)}) async-start(), calls=%async_computation.14 | async-start | bytes 5505024 | tf_op jit(solution)/shard_map/all_gather | solution.py:97
  388.1 101.2 %copy-start.30 = (f32[576]{0:T(1024)S(1)}, f32[576]{0:T(1024)}, u32[]{:S(2)}) copy-start(f32[576]{0:T(1024)} %param.28) | copy-start | bytes 6916
  388.1 93.9 %reduce-scatter.16.cloned.1.call-start = ((), (), s32[]{:S(2)}) async-start(), calls=%async_computation.15 | async-start | bytes 1474560 | tf_op jit(solution)/shard_map/reduce_scatter | solution.py:99
  448.1 74.2 %all-gather.16.cloned.1.call-start = ((), (), s32[]{:S(2)}) async-start(), calls=%async_computation.16 | async-start | bytes 1474560 | tf_op jit(solution)/shard_map/all_gather | solution.py:88
  498.4 120.5 %reduce-scatter.18.cloned.1.call-start = ((), (), s32[]{:S(2)}) async-start(), calls=%async_computation.17 | async-start | bytes 11010048 | tf_op jit(solution)/shard_map/reduce_scatter | solution.py:93
  529.0 191.4 %all-gather.18.cloned.1.call-start = ((), (), s32[]{:S(2)}) async-start(), calls=%async_computation.18 | async-start | bytes 10616832 | tf_op jit(solution)/shard_map/all_gather | solution.py:97
  627.5 136.5 %copy-start.5 = (bf16[256,576]{0,1:T(8,128)(2,1)S(1)}, bf16[256,576]{0,1:T(8,128)(2,1)}, u32[]{:S(2)}) copy-start(bf16[256,576]{0,1:T(8,128)(2,1)} %reduce-scatter.12.cloned.1.call-done) | copy-start | bytes 884740
  627.5 136.5 %copy-start.37 = (f32[256]{0:T(256)S(1)}, f32[256]{0:T(256)}, u32[]{:S(2)}) copy-start(f32[256]{0:T(256)} %copy-done.36) | copy-start | bytes 3076
  627.5 136.5 %copy-start.49 = (f32[256]{0:T(256)S(1)}, f32[256]{0:T(256)}, u32[]{:S(2)}) copy-start(f32[256]{0:T(256)} %copy-done.48) | copy-start | bytes 3076
  627.5 141.8 %copy-start.56 = (f32[256]{0:T(256)S(1)}, f32[256]{0:T(256)}, u32[]{:S(2)}) copy-start(f32[256]{0:T(256)} %psum.149) | copy-start | bytes 3076
  627.5 141.8 %copy-start.50 = (f32[256]{0:T(256)S(1)}, f32[256]{0:T(256)}, u32[]{:S(2)}) copy-start(f32[256]{0:T(256)} %dynamic-slice_convert_fusion) | copy-start | bytes 3076
  627.5 141.8 %copy-start.52 = (f32[256]{0:T(256)S(1)}, f32[256]{0:T(256)}, u32[]{:S(2)}) copy-start(f32[256]{0:T(256)} %copy-done.51) | copy-start | bytes 3076
  627.5 136.5 %reduce-scatter.20.cloned.1.call-start = ((), (), s32[]{:S(2)}) async-start(), calls=%async_computation.19 | async-start | bytes 1474560 | tf_op jit(solution)/shard_map/reduce_scatter | solution.py:99
  730.1 39.3 %copy-start.7 = (bf16[256,576]{0,1:T(8,128)(2,1)S(1)}, bf16[256,576]{0,1:T(8,128)(2,1)}, u32[]{:S(2)}) copy-start(bf16[256,576]{0,1:T(8,128)(2,1)} %reduce-scatter.16.cloned.1.call-done) | copy-start | bytes 884740
  730.1 39.3 %copy-start.12 = (bf16[256,576]{0,1:T(8,128)(2,1)S(1)}, bf16[256,576]{0,1:T(8,128)(2,1)}, u32[]{:S(2)}) copy-start(bf16[256,576]{0,1:T(8,128)(2,1)} %param.31) | copy-start | bytes 884740
  730.1 45.9 %copy-start.55 = (f32[256]{0:T(256)S(1)}, f32[256]{0:T(256)}, u32[]{:S(2)}) copy-start(f32[256]{0:T(256)} %psum.148) | copy-start | bytes 3076
  730.1 70.6 %all-gather.20.cloned.1.call-start = ((), (), s32[]{:S(2)}) async-start(), calls=%async_computation.20 | async-start | bytes 1474560 | tf_op jit(solution)/shard_map/all_gather | solution.py:88
  765.4 35.3 %copy-start.19 = (bf16[256,576]{0,1:T(8,128)(2,1)S(1)}, bf16[256,576]{0,1:T(8,128)(2,1)}, u32[]{:S(2)}) copy-start(bf16[256,576]{0,1:T(8,128)(2,1)} %param.21) | copy-start | bytes 884740
  776.8 26.8 %copy-start.64 = (f32[512]{0:T(512)S(1)}, f32[512]{0:T(512)}, u32[]{:S(2)}) copy-start(f32[512]{0:T(512)} %copy-done.63) | copy-start | bytes 6148
  776.8 26.8 %copy-start.66 = (f32[512]{0:T(512)S(1)}, f32[512]{0:T(512)}, u32[]{:S(2)}) copy-start(f32[512]{0:T(512)} %copy-done.65) | copy-start | bytes 6148
  776.8 48.6 %reduce-scatter.22.cloned.1.call-start = ((), (), s32[]{:S(2)}) async-start(), calls=%async_computation.21 | async-start | bytes 1572864 | tf_op jit(solution)/shard_map/reduce_scatter | solution.py:93
  803.6 76.5 %reduce-scatter.24.cloned.1.call-start = ((), (), s32[]{:S(2)}) async-start(), calls=%async_computation.22 | async-start | bytes 1179648 | tf_op jit(solution)/shard_map/reduce_scatter | solution.py:280
  826.6 2.6 copy-start.3
  830.9 3.0 copy-start.10
  830.9 3.0 copy-start.58
  831.6 2.8 copy-start.35
  845.0 6.3 copy-start.21
  845.0 6.3 copy-start.23
  845.1 82.5 %reduce-scatter.26.cloned.1.call-start = ((), (), s32[]{:S(2)}) async-start(), calls=%async_computation.23 | async-start | bytes 1474560 | tf_op jit(solution)/shard_map/reduce_scatter | solution.py:99
  845.3 6.1 copy-start.11
  853.3 38.4 %copy-start.25 = (bf16[576,64]{1,0:T(8,128)(2,1)S(1)}, bf16[576,64]{1,0:T(8,128)(2,1)}, u32[]{:S(2)}) copy-start(bf16[576,64]{1,0:T(8,128)(2,1)} %copy-done.24) | copy-start | bytes 221188
  853.3 38.4 %copy-start.27 = (bf16[576,64]{1,0:T(8,128)(2,1)S(1)}, bf16[576,64]{1,0:T(8,128)(2,1)}, u32[]{:S(2)}) copy-start(bf16[576,64]{1,0:T(8,128)(2,1)} %copy-done.26) | copy-start | bytes 221188
  894.5 169.3 %all-reduce.8.cloned.1.call-start = ((), (), s32[]{:S(2)}) async-start(), calls=%async_computation.25 | async-start | bytes 14155776 | tf_op jit(solution)/shard_map/psum | solution.py:304
  902.4 3.0 copy-start.15
  902.4 4.3 copy-start.68
  909.0 18.6 %copy-start.31 = (f32[576]{0:T(1024)S(1)}, f32[576]{0:T(1024)}, u32[]{:S(2)}) copy-start(f32[576]{0:T(1024)} %param.25) | copy-start | bytes 6916
  909.0 18.6 %copy-start.45 = (f32[256]{0:T(256)S(1)}, f32[256]{0:T(256)}, u32[]{:S(2)}) copy-start(f32[256]{0:T(256)} %copy-done.44) | copy-start | bytes 3076
  909.0 94.1 %copy-start.54 = (f32[256]{0:T(256)S(1)}, f32[256]{0:T(256)}, u32[]{:S(2)}) copy-start(f32[256]{0:T(256)} %copy-done.53) | copy-start | bytes 3076
  1070.9 4.0 copy-start.14
  1074.9 2.3 copy-start.13
  1077.2 2.3 copy-start.1
  (23 other events, 26.7 us)
Sparse Core Ops, SparseCore 0:
  15.2 25.5 all-gather.9
  44.4 27.4 reduce-scatter.9
  74.3 34.7 all-gather.21
  136.4 31.8 reduce-scatter.11
  183.9 23.7 all-gather.11
  219.5 162.7 reduce-scatter.13
  388.2 54.3 all-gather.13
  448.2 33.7 reduce-scatter.15
  498.5 23.6 all-gather.15
  529.1 89.7 reduce-scatter.17
  627.6 92.7 all-gather.17
  730.2 33.7 reduce-scatter.19
  776.9 23.6 all-gather.19
  803.7 21.6 reduce-scatter.21
  845.2 34.9 reduce-scatter.23
  894.6 32.9 reduce-scatter.25
  933.5 130.3 all-reduce.7
where the time goes:
time: 1090 us
  waiting for transfers between devices  774 us (71%)
  blocking collectives  120 us (11%)
  other arithmetic  68.6 us (6%)
  matrix products  66.6 us (6%)
  local copies, waits for them, and re-layouts  39.6 us (4%)
  between operations  15.1 us (1%)
    reduce_scatter x4, waiting for transfers between devices, lift_rows(): lax.psum_scatter(transform(gathered), 'row', scatter_dimension=0, tiled=T...  302 us
    all_gather x2, waiting for transfers between devices, sink_rows(): gathered = lax.all_gather(low_rows, 'row', axis=0, tiled=True)  147 us
    reduce_scatter x4, waiting for transfers between devices, sink_rows(): lax.psum_scatter(transform(gathered).astype(jnp.bfloat16), 'col', scatter...  114 us
    all_gather x4, waiting for transfers between devices, spread_cols(): return lax.all_gather(low_rows, 'col', axis=0, tiled=True)  94.8 us
    psum x1, blocking collectives, body(): lax.psum((placed(grad_gain_attn_in), placed(grad_gain_attn_out), placed(g...  67.4 us
    psum x1, waiting for transfers between devices, body(): lax.psum(grad_w_key.astype(jnp.bfloat16), 'dp').astype(jnp.float32)  58.8 us
    psum x8, blocking collectives, row_total(): return lax.psum(values, 'row')  33.9 us
    all_gather x1, waiting for transfers between devices, body(): lax.all_gather(key_value_piece[None], ('row', 'col'), axis=0, tiled=True)  30.9 us
  transfers between devices with their start and end apart: 17, of which 17 were waited for; matrix products, arithmetic and copies ran while one was open for 4% of the time, Pallas kernels for 0%

commit v1 on v0

v1 whole, which is shorter than its diff:
```python
import jax
import jax.numpy as jnp
from jax import lax
from jax.sharding import PartitionSpec as P

WINDOW = 512
EPSILON = 1e-06
ROPE_BASE = 10000.0
MASKED = -1e30
GROUP = ("row", "col")
BF = jnp.bfloat16
F32 = jnp.float32
OWN = 128
D = 1152
HALF = 576
HIDDEN = 864
ROW_PART = 36
BLOCKS = ((0, 0), (0, 1), (2, 0), (2, 1), (1, 0), (1, 1), (3, 0), (3, 1))


def member(z, core):
    return (z % 2) * 4 + (z // 2) * 2 + core


def z_pairs(step):
    return [(member(z, c), member((z + step) % 4, c)) for z in range(4) for c in range(2)]


CORE_PAIRS = [(member(z, c), member(z, 1 - c)) for z in range(4) for c in range(2)]
ROW_PAIRS = [(0, 1), (1, 0)]


def move_z(values, step):
    return lax.ppermute(values, GROUP, z_pairs(step % 4))


def move_core(values):
    return lax.ppermute(values, GROUP, CORE_PAIRS)


def move_row(values):
    return lax.ppermute(values, "row", ROW_PAIRS)


def move_plane(values, axis, step):
    if axis == "x":
        pairs = [(x * 4 + y, ((x + step) % 4) * 4 + y) for x in range(4) for y in range(4)]
    else:
        pairs = [(x * 4 + y, x * 4 + (y + step) % 4) for x in range(4) for y in range(4)]
    return lax.ppermute(values, "dp", pairs)


def gather_blocks(own, steps):
    held = {0: own}
    for step in steps:
        held[step] = move_z(own, step)
    order = [0] + [s for s in (2, 1, 3) if s in steps]
    swapped = {0: move_core(own)}
    for step in (s for s in (1, 3, 2) if s in steps):
        swapped[step] = move_core(held[step])
    pieces = []
    for step in order:
        pieces += [held[step], swapped[step]]
    return jnp.concatenate(pieces, axis=0)


def reduce_blocks(partial, steps):
    order = [0] + [s for s in (2, 1, 3) if s in steps]
    rows = partial.shape[0] // (2 * len(order))
    blocks = partial.reshape(len(order), 2, rows, partial.shape[1])
    total = None
    arrived = []
    for at in reversed(range(len(order))):
        swapped = move_core(blocks[at, 1].astype(BF)).astype(F32)
        both = blocks[at, 0].astype(F32) + swapped
        if at == 0:
            total = both
        else:
            arrived.append(move_z(both.astype(BF), -order[at]))
    for piece in arrived:
        total = total + piece.astype(F32)
    return total


def reduce_ring(parts, coordinate, axis):
    total = lax.dynamic_index_in_dim(parts, coordinate, 0, keepdims=False).astype(F32)
    for step in (1, 3, 2):
        sent = lax.dynamic_index_in_dim(parts, (coordinate + step) % 4, 0, keepdims=False)
        total = total + move_plane(sent, axis, step).astype(F32)
    return total.astype(BF)


def gather_ring(part, coordinate, axis):
    result = jnp.zeros((4,) + part.shape, part.dtype)
    result = lax.dynamic_update_index_in_dim(result, part, coordinate, 0)
    for step in (1, 3, 2):
        got = move_plane(part, axis, step)
        result = lax.dynamic_update_index_in_dim(result, got, (coordinate + 4 - step) % 4, 0)
    return result


def reduce_plane(values, at, first, second):
    rows, width = values.shape
    once = reduce_ring(values.reshape(4, rows // 4, width), at[first], first)
    return reduce_ring(once.reshape(4, rows // 16, width), at[second], second)


def gather_plane(part, at, first, second):
    rows, width = part.shape
    once = gather_ring(part, at[second], second).reshape(4 * rows, width)
    return gather_ring(once, at[first], first).reshape(16 * rows, width)


def layout(lengths_row, places):
    slot_count = lengths_row.shape[0]
    seq_ends = jnp.cumsum(lengths_row)
    sequence = jnp.sum((places[:, None] >= seq_ends[None, :]).astype(jnp.int32), axis=1)
    starts = jnp.concatenate([jnp.zeros((1,), jnp.int32), seq_ends])
    labels = jnp.arange(slot_count + 1, dtype=jnp.int32)
    start_of = jnp.sum(jnp.where(sequence[:, None] == labels[None, :], starts[None, :], 0), axis=1)
    live_rows = (places < seq_ends[slot_count - 1]).astype(jnp.int32)
    return (sequence, places - start_of, live_rows)


def rotation(positions, full_width):
    half_width = full_width // 2
    frequency = ROPE_BASE ** (-2.0 * jnp.arange(half_width, dtype=F32) / full_width)
    angles = positions.astype(F32)[:, None] * frequency
    return (jnp.cos(angles), jnp.sin(angles))


def rotate(values, cosine, sine):
    half_width = values.shape[1] // 2
    first, second = values[:, :half_width], values[:, half_width:]
    return jnp.concatenate(
        [first * cosine - second * sine, second * cosine + first * sine], axis=1
    )


def inverse_of(values):
    return lax.rsqrt(jnp.mean(values * values, axis=1, keepdims=True) + EPSILON)


def norm_back(values, inverse, gain, incoming):
    inner = jnp.mean(incoming * gain * values, axis=1, keepdims=True)
    return inverse * gain * incoming - values * (inverse * inverse * inverse * inner)


def dot(left, right, left_dim=1, right_dim=0):
    return lax.dot_general(
        left, right, (((left_dim,), (right_dim,)), ((), ())), preferred_element_type=F32
    )


def body(
    tokens,
    doc_lengths,
    w_query,
    w_key,
    w_value,
    w_out,
    w_gate,
    w_up,
    w_down,
    gain_attn_in,
    gain_attn_out,
    gain_ff_in,
    gain_ff_out,
    gain_query,
    gain_key,
    cotangent,
):
    row = lax.axis_index("row")
    col = lax.axis_index("col")
    plane = lax.axis_index("dp")
    at = {"x": plane // 4, "y": plane % 4}
    z, core = (col // 2) * 2 + row, col % 2
    head_dim = gain_query.shape[0]
    score_scale = head_dim ** (-0.5)

    def in_order(own, other, axis):
        return jnp.where(
            row == 0,
            jnp.concatenate([own, other], axis=axis),
            jnp.concatenate([other, own], axis=axis),
        )

    def whole_rows(block):
        halves = block.reshape(2, OWN, HALF)
        other = move_row(lax.dynamic_index_in_dim(halves, 1 - row, 0, keepdims=False))
        return in_order(lax.dynamic_index_in_dim(halves, row, 0, keepdims=False), other, 1)

    def split_rows(owned, sent):
        halves = owned.reshape(OWN, 2, HALF)
        sent_halves = sent.reshape(OWN, 2, HALF)
        other = move_row(lax.dynamic_index_in_dim(sent_halves, 1 - row, 1, keepdims=False))
        own = lax.dynamic_index_in_dim(halves, row, 1, keepdims=False)
        return in_order(own, other.astype(own.dtype), 0)

    def half_of(vector):
        return lax.dynamic_slice_in_dim(vector, row * HALF, HALF, 0)

    residual = whole_rows(tokens).astype(F32)
    gain_pack = jnp.stack([gain_attn_in, gain_attn_out, gain_ff_in, gain_ff_out], 0)
    gain_all = in_order(gain_pack, move_row(gain_pack), 1)
    full_attn_in, full_attn_out, full_ff_in, full_ff_out = (gain_all[i : i + 1] for i in range(4))

    inverse_in = inverse_of(residual)
    normed_own = (residual * inverse_in * full_attn_in).astype(BF)
    normed_in = gather_blocks(normed_own, (1, 3, 2))

    query_weights = in_order(w_query, move_row(w_query), 0)
    kv_own = jnp.concatenate([w_key, w_value], axis=1)
    kv_blocks = gather_blocks(kv_own[None], (1, 3, 2))
    owner_row = jnp.stack([((z - k) % 4) % 2 for k, d in BLOCKS])
    owner_col = jnp.stack([((z - k + 4) % 4) // 2 * 2 + (core + d) % 2 for k, d in BLOCKS])
    owner = owner_row * 4 + owner_col
    place_of = jnp.sum(
        jnp.where(owner[None, :] == jnp.arange(8)[:, None], jnp.arange(8)[None, :], 0), axis=1
    )
    kv_weights = (
        jnp.take(kv_blocks, place_of, axis=0)
        .reshape(2, 4, HALF, 2, 64)
        .transpose(0, 2, 3, 1, 4)
        .reshape(D, 512)
    )
    out_weights = in_order(w_out, move_row(w_out), 1)

    stacked = jnp.stack([w_gate, w_up, w_down.T], axis=0)
    piece = lax.dynamic_slice(
        stacked, (0, plane * ROW_PART, (1 - row) * HIDDEN), (3, ROW_PART, HIDDEN)
    )
    gathered = lax.all_gather(move_row(piece), "dp", axis=0, tiled=False)
    other_half = gathered.transpose(1, 0, 2, 3).reshape(3, HALF, HIDDEN)
    own_half = lax.dynamic_slice_in_dim(stacked, row * HIDDEN, HIDDEN, 2)
    ff_weights = in_order(own_half, other_half, 1)
    gate_weights, up_weights, down_weights = ff_weights[0], ff_weights[1], ff_weights[2]

    starts = owner_col * 256 + owner_row * OWN
    places = (starts[:, None] + jnp.arange(OWN, dtype=jnp.int32)[None, :]).reshape(-1)
    sequence, positions, live_rows = layout(doc_lengths[0], places)
    live_own = live_rows[:OWN].astype(F32)[:, None]
    cosine, sine = rotation(positions, head_dim)
    q_rows = 512
    q_cosine, q_sine = cosine[:q_rows], sine[:q_rows]
    distance = positions[:q_rows, None] - positions[None, :]
    allowed = (
        (sequence[:q_rows, None] == sequence[None, :]) & (distance >= 0) & (distance < WINDOW)
    )

    pre_query = dot(normed_in[:q_rows], query_weights)
    key_value = dot(normed_in, kv_weights).astype(BF)
    pre_key = key_value[:, :head_dim].astype(F32)
    values_low = key_value[:, head_dim:]
    inverse_q = inverse_of(pre_query)
    inverse_k = inverse_of(pre_key)
    queries_low = rotate(pre_query * inverse_q * gain_query[None], q_cosine, q_sine).astype(BF)
    keys_low = rotate(pre_key * inverse_k * gain_key[None], cosine, sine).astype(BF)
    scores = jnp.where(allowed, dot(queries_low, keys_low, 1, 1) * score_scale, MASKED)
    highest = jnp.max(scores, axis=1, keepdims=True)
    weights = jnp.exp(scores - highest)
    totals = jnp.sum(weights, axis=1, keepdims=True)
    shares = weights / totals
    shares_low = shares.astype(BF)
    attended = dot(shares_low, values_low).astype(BF)

    branch_attn = reduce_blocks(dot(attended, out_weights), (2,))
    inverse_attn_out = inverse_of(branch_attn)
    hidden_mid = residual + branch_attn * inverse_attn_out * full_attn_out
    inverse_ff_in = inverse_of(hidden_mid)
    normed_ff = gather_blocks((hidden_mid * inverse_ff_in * full_ff_in).astype(BF), (1, 3, 2))

    gate = dot(normed_ff, gate_weights)
    upward = dot(normed_ff, up_weights)
    activated, activate_back = jax.vjp(
        lambda gate_part, upward_part: jax.nn.gelu(gate_part, approximate=True) * upward_part,
        gate,
        upward,
    )
    activated_low = activated.astype(BF)
    branch_ff = reduce_blocks(dot(activated_low, down_weights, 1, 1), (1, 3, 2))
    inverse_ff_out = inverse_of(branch_ff)
    mixed_own = (hidden_mid + branch_ff * inverse_ff_out * full_ff_out).astype(BF)

    grad_result = whole_rows(cotangent).astype(F32) * live_own
    gain_sum_ff_out = jnp.sum(grad_result * branch_ff * inverse_ff_out, axis=0)
    grad_branch_ff = norm_back(branch_ff, inverse_ff_out, full_ff_out, grad_result).astype(BF)
    grad_branch_all = gather_blocks(grad_branch_ff, (1, 3, 2))
    grad_activated = dot(grad_branch_all, down_weights)
    grad_gate, grad_up = activate_back(grad_activated)
    grad_gate, grad_up = grad_gate.astype(BF), grad_up.astype(BF)
    grad_normed_ff = reduce_blocks(
        dot(grad_gate, gate_weights, 1, 1) + dot(grad_up, up_weights, 1, 1), (1, 3, 2)
    )
    part_down = dot(grad_branch_all, activated_low, 0, 0).astype(BF)
    part_gate = dot(normed_ff, grad_gate, 0, 0).astype(BF)
    part_up = dot(normed_ff, grad_up, 0, 0).astype(BF)

    grad_hidden = grad_result + norm_back(hidden_mid, inverse_ff_in, full_ff_in, grad_normed_ff)
    gain_sum_attn_out = jnp.sum(grad_hidden * branch_attn * inverse_attn_out, axis=0)
    grad_branch_attn = norm_back(
        branch_attn, inverse_attn_out, full_attn_out, grad_hidden
    ).astype(BF)
    grad_attn_all = gather_blocks(grad_branch_attn, (2,))
    grad_attended = dot(grad_attn_all, out_weights, 1, 1).astype(BF)
    part_out = dot(grad_attn_all, attended, 0, 0)

    grad_shares = dot(grad_attended, values_low, 1, 1)
    inner = jnp.sum(shares * grad_shares, axis=1, keepdims=True)
    grad_scores = (shares * (grad_shares - inner) * score_scale).astype(BF)
    grad_query = dot(grad_scores, keys_low)
    grad_key = dot(grad_scores, queries_low, 0, 0)
    grad_value = dot(shares_low, grad_attended, 0, 0)
    turned_q = rotate(grad_query, q_cosine, -q_sine)
    turned_k = rotate(grad_key, cosine, -sine)
    gain_sum_query = jnp.sum(turned_q * pre_query * inverse_q, axis=0)
    gain_sum_key = jnp.sum(turned_k * pre_key * inverse_k, axis=0)
    grad_pre_query = norm_back(pre_query, inverse_q, gain_query[None], turned_q).astype(BF)
    grad_pre_key = norm_back(pre_key, inverse_k, gain_key[None], turned_k)
    grad_kv = jnp.concatenate([grad_pre_key, grad_value], axis=1).astype(BF)

    from_kv = dot(grad_kv, kv_weights, 1, 1)
    from_query = dot(grad_pre_query, query_weights, 1, 1)
    grad_normed_in = reduce_blocks(
        jnp.concatenate([from_kv[:q_rows] + from_query, from_kv[q_rows:]], axis=0), (1, 3, 2)
    )
    grad_tokens_own = grad_hidden + norm_back(residual, inverse_in, full_attn_in, grad_normed_in)

    mixed = split_rows(mixed_own, mixed_own)
    grad_tokens = split_rows(grad_tokens_own, grad_tokens_own.astype(BF))

    parts = jnp.concatenate([part_gate, part_up, part_down], axis=1)
    halves = parts.reshape(2, HALF, 3 * HIDDEN)
    own_part = lax.dynamic_index_in_dim(halves, row, 0, keepdims=False)
    other_part = lax.dynamic_index_in_dim(halves, 1 - row, 0, keepdims=False)
    own_piece = reduce_plane(own_part, at, "x", "y")
    peer_piece = move_row(reduce_plane(other_part, at, "y", "x"))
    own_sum = gather_plane(own_piece, at, "x", "y").astype(F32)
    peer_sum = gather_plane(peer_piece, at, "y", "x").astype(F32)

    def both_blocks(i):
        cut = slice(i * HIDDEN, (i + 1) * HIDDEN)
        return in_order(own_sum[:, cut], peer_sum[:, cut], 1)

    grad_w_gate, grad_w_up, grad_w_down = both_blocks(0), both_blocks(1), both_blocks(2).T

    part_query = dot(normed_in[:q_rows], grad_pre_query, 0, 0)
    pair = jnp.concatenate([part_query, part_out], axis=1).reshape(2, HALF, 512)
    pair_own = lax.dynamic_index_in_dim(pair, row, 0, keepdims=False)
    pair_other = lax.dynamic_index_in_dim(pair, 1 - row, 0, keepdims=False).astype(BF)
    pair_sum = (pair_own + move_row(pair_other).astype(F32)).astype(BF)
    part_kv = (
        dot(normed_in, grad_kv, 0, 0)
        .reshape(2, HALF, 2, 4, 64)
        .transpose(0, 3, 1, 2, 4)
        .reshape(8, HALF, 128)
    )
    kv_sum = reduce_blocks(
        jnp.take(part_kv, owner, axis=0).reshape(8 * HALF, 128), (1, 3, 2)
    ).astype(BF)
    first = pair_sum[:, 256:]
    second = jnp.concatenate([pair_sum[:, :256], kv_sum], axis=1)
    first_sum = gather_plane(reduce_plane(first, at, "x", "y"), at, "x", "y").astype(F32)
    second_sum = gather_plane(reduce_plane(second, at, "y", "x"), at, "y", "x").astype(F32)
    grad_w_query = second_sum[:, :256]
    grad_w_key = second_sum[:, 256:320]
    grad_w_value = second_sum[:, 320:384]
    grad_w_out = first_sum.T

    def over_cols(vector):
        vector = vector + move_core(vector)
        return vector + move_z(vector, 2)

    products_ff = jnp.sum(grad_w_gate * w_gate.astype(F32), axis=1) + jnp.sum(
        grad_w_up * w_up.astype(F32), axis=1
    )
    products_in = (
        jnp.sum(grad_w_query * w_query.astype(F32), axis=1)
        + jnp.sum(grad_w_key * w_key.astype(F32), axis=1)
        + jnp.sum(grad_w_value * w_value.astype(F32), axis=1)
    )
    products = over_cols(jnp.stack([products_ff, products_in]))
    grad_gain_ff_in = products[0] / gain_ff_in
    grad_gain_attn_in = products[1] / gain_attn_in

    packed = jnp.concatenate(
        [gain_sum_ff_out, gain_sum_attn_out, gain_sum_query, gain_sum_key]
    ).reshape(22, 128)
    for axis in ("x", "y"):
        packed = (packed + move_plane(packed, axis, 2)) + (
            move_plane(packed, axis, 1) + move_plane(packed, axis, 3)
        )
    packed = packed + move_core(packed)
    packed = (packed + move_z(packed, 2)) + (move_z(packed, 1) + move_z(packed, 3))
    packed = packed.reshape(-1)
    return (
        mixed,
        grad_tokens,
        grad_w_query,
        grad_w_key,
        grad_w_value,
        grad_w_out,
        grad_w_gate,
        grad_w_up,
        grad_w_down,
        grad_gain_attn_in,
        half_of(packed[D : 2 * D]),
        grad_gain_ff_in,
        half_of(packed[:D]),
        packed[2 * D : 2 * D + head_dim],
        packed[2 * D + head_dim :],
    )


def solution(mesh):
    return jax.shard_map(
        body,
        mesh=mesh,
        in_specs=(
            P(("dp", "col"), "row"),
            P("dp", None),
            P("row", "col"),
            P("row", "col"),
            P("row", "col"),
            P("col", "row"),
            P("row", "col"),
            P("row", "col"),
            P("col", "row"),
            P("row"),
            P("row"),
            P("row"),
            P("row"),
            P(),
            P(),
            P(("dp", "col"), "row"),
        ),
        out_specs=(
            P(("dp", "col"), "row"),
            P(("dp", "col"), "row"),
            P("row", "col"),
            P("row", "col"),
            P("row", "col"),
            P("col", "row"),
            P("row", "col"),
            P("row", "col"),
            P("col", "row"),
            P("row"),
            P("row"),
            P("row"),
            P("row"),
            P(),
            P(),
        ),
        check_vma=False,
    )
```

time: 1090 us -> 672 us (0.62)
  waiting for transfers between devices: 774 us -> 125 us
  starting transfers between devices: 1.46 us -> 180 us
  local copies, waits for them, and re-layouts: 39.6 us -> 177 us
  blocking collectives: 120 us -> 0 us
  other arithmetic: 68.6 us -> 95.3 us
    reduce_scatter x9 -> x0, waiting for transfers between devices: 443 us -> none  [the longest x4 302 us: lift_rows(): lax.psum_scatter(transform(gathered), 'row', scatter_dimension=0, tiled=T...]
    all_gather x7 -> x1, waiting for transfers between devices: 273 us -> 0.01 us  [body(): gathered = lax.all_gather(move_row(piece), 'dp', axis=0, tiled=False)]
    ppermute x0 -> x132, starting transfers between devices: none -> 180 us  [the longest x38 68.4 us: move_core(): return lax.ppermute(values, GROUP, CORE_PAIRS)]
    ppermute x0 -> x132, waiting for transfers between devices: none -> 125 us  [the longest x54 64.8 us: move_plane(): return lax.ppermute(values, 'dp', pairs)]
    psum x9 -> x0, blocking collectives: 101 us -> none  [the longest x1 67.4 us: body(): lax.psum((placed(grad_gain_attn_in), placed(grad_gain_attn_out), placed(g...]
    psum x1 -> x0, waiting for transfers between devices: 58.8 us -> none  [body(): lax.psum(grad_w_key.astype(jnp.bfloat16), 'dp').astype(jnp.float32)]
    unnamed x145 -> x249, local copies, waits for them, and re-layouts: 11.9 us -> 53.7 us
    reshape x2 -> x15, local copies, waits for them, and re-layouts: 3.38 us -> 28.1 us  [the longest x2 11.3 us: body(): other_half = gathered.transpose(1, 0, 2, 3).reshape(3, HALF, HIDDEN)]
  transfers between devices with their start and end apart: 17 -> 133, of which waited for: 17 -> 38; matrix products, arithmetic and copies ran while one was open for 4% -> 34% of each run, Pallas kernels for 0% -> 0%
where the time goes in v1:
time: 672 us; the launch traced here: 660 us
  starting transfers between devices  180 us (27%)
  local copies, waits for them, and re-layouts  177 us (26%)
  waiting for transfers between devices  125 us (19%)
  other arithmetic  95.3 us (14%)
  matrix products  66.6 us (10%)
  between operations  16.9 us (3%)
    ppermute x38, starting transfers between devices, move_core(): return lax.ppermute(values, GROUP, CORE_PAIRS)  68.4 us
    dot_general x24, matrix products, dot(): lax.dot_general(left, right, (((left_dim,), (right_dim,)), ((), ())), pre...  66.6 us
    ppermute x54, waiting for transfers between devices, move_plane(): return lax.ppermute(values, 'dp', pairs)  64.8 us
    ppermute x54, starting transfers between devices, move_plane(): return lax.ppermute(values, 'dp', pairs)  62.1 us
    unnamed x249, local copies, waits for them, and re-layouts  53.7 us
    ppermute x30, starting transfers between devices, move_z(): return lax.ppermute(values, GROUP, z_pairs(step % 4))  40.4 us
    ppermute x30, waiting for transfers between devices, move_z(): return lax.ppermute(values, GROUP, z_pairs(step % 4))  34.2 us
    ppermute x10, waiting for transfers between devices, move_row(): return lax.ppermute(values, 'row', ROW_PAIRS)  24.6 us
  transfers between devices with their start and end apart: 133, of which 38 were waited for; matrix products, arithmetic and copies ran while one was open for 34% of the time, Pallas kernels for 0%

profile of v1, /device:TPU:1, one launch (start us, length us, event | category | flops | bytes accessed | tf_op | source)
XLA Modules:
  0.0 660.3 jit_solution(6259516625896791875)
XLA Ops:
  8.8 4.4 collective-permute-start.11
  24.9 3.5 copy.117
  28.4 4.1 copy.118
  32.5 4.1 copy.119
  36.6 3.5 pad_maximum_fusion
  40.2 2.8 copy-done
  46.4 3.3 collective-permute-done
  57.8 3.6 collective-permute-done.28
  70.5 2.7 collective-permute-start.8
  90.8 3.2 convolution_convert_fusion.3
  106.4 3.1 collective-permute-start.20
  109.5 6.8 %collective-permute-done.20 = bf16[128,1152]{1,0:T(8,128)(2,1)S(1)} collective-permute-done((bf16[128,1152]{1,0:T(8,128)(2,1)S(1)}, bf16[128,1152]{1,0:T(8,128)(2,1)S(1)}, u32[]{:S(2)}, u32[]{:S(2)}) %collective-permute-start.20) | collective-permute-done | bytes 294944 | tf_op jit(solution)/shard_map/ppermute | solution.py:34
  117.8 3.2 collective-permute-start.22
  126.4 3.9 constant_dynamic-slice_fusion.3
  130.7 4.3 collective-permute-done.24
  135.5 12.5 %collective-permute-start.27 = (bf16[128,1152]{1,0:T(8,128)(2,1)S(1)}, bf16[128,1152]{1,0:T(8,128)(2,1)S(1)}, u32[]{:S(2)}, u32[]{:S(2)}) collective-permute-start(bf16[128,1152]{1,0:T(8,128)(2,1)S(1)} %collective-permute-done.26), channel_id=1, source_target_pairs={{0,1},{1,0},{4,5},{5,4},{2,3},{3,2},{6,7},{7,6},{8,9},{9,8},{12,13... | collective-permute-start | bytes 884744 | tf_op jit(solution)/shard_map/ppermute | solution.py:38
  153.2 4.0 copy.149
  157.2 5.8 reshape.989
  163.0 5.6 copy.122
  168.6 9.9 %maximum_select_fusion = bf16[3,1152,864]{1,2,0:T(8,128)(2,1)S(1)} fusion(bf16[3,576,864]{1,2,0:T(8,128)(2,1)} %copy.122, bf16[3,576,864]{1,2,0:T(8,128)(2,1)} %constant_dynamic-slice_fusion.3, pred[]{:T(512)S(6)} %eq.135), kind=kLoop, calls=%fused_computation.3 | loop fusion | flops 26873856 | bytes 11943937 | tf_op jit(solution)/shard_map/jit(_where)/select_n | solution.py:182
  178.5 5.9 fusion.18
  184.5 8.3 %multiply_convert_fusion.1 = (bf16[1024,864]{0,1:T(8,128)(2,1)}, f32[1024,864]{0,1:T(8,128)}) fusion(f32[1024,864]{0,1:T(8,128)S(1)} %fusion.18, bf16[1024,1152]{1,0:T(8,128)(2,1)} %constant_dynamic-update-slice_fusion.16, bf16[3,1152,864]{1,2,0:T(8,128)(2,1)S(1)} %maximum_select_fusion), kind=kOutput, calls=%fused_computation.23 | convolution fusion | flops 2047279104 | bytes 13197312 | tf_op jit(solution)/shard_map/dot_general | solution.py:150
  192.7 4.5 dot_general.81
  197.2 4.5 fusion.175
  212.4 5.8 collective-permute-done.31
  218.2 5.2 collective-permute-done.33
  229.8 3.2 collective-permute-start.41
  237.0 12.9 %collective-permute-done.36 = bf16[128,576]{0,1:T(8,128)(2,1)S(1)} collective-permute-done((bf16[128,576]{0,1:T(8,128)(2,1)S(1)}, bf16[128,576]{0,1:T(8,128)(2,1)S(1)}, u32[]{:S(2)}, u32[]{:S(2)}) %collective-permute-start.36) | collective-permute-done | bytes 147488 | tf_op jit(solution)/shard_map/ppermute | solution.py:42
  260.5 8.1 %multiply_convert_fusion = (bf16[1024,864]{0,1:T(8,128)(2,1)S(1)}, bf16[1024,864]{0,1:T(8,128)(2,1)S(1)}) fusion(f32[1024,864]{0,1:T(8,128)S(1)} %copy-done.104, f32[1024,864]{0,1:T(8,128)} %get-tuple-element.220, bf16[1024,1152]{1,0:T(8,128)(2,1)} %constant_dynamic-update-slice_fusion.24, bf16[3,1152,864]{1,2,0:T(8,128)(2,1)} %copy-done.3), kind=kOutput, calls=%fused_computation.22 | convolution fusion | flops 2059665408 | bytes 14966784 | tf_op jit(solution)/shard_map/dot_general | solution.py:150
  268.6 2.9 fusion.17
  271.5 4.3 convolution_convert_fusion.2
  278.3 4.3 convolution_convert_fusion.1
  282.6 4.6 bitcast_convert_fusion.3
  289.1 3.2 pad_maximum_fusion.1
  292.3 9.3 %copy.134 = bf16[1152,2592]{1,0:T(8,128)(2,1)} copy(bf16[1152,2592]{0,1:T(8,128)(2,1)} %pad_maximum_fusion.1) | data formatting | bytes 11943936 | tf_op jit(solution)/shard_map/concatenate | solution.py:332
  301.6 3.4 constant_dynamic-slice_fusion
  314.0 9.6 %collective-permute-done.47 = bf16[128,1152]{1,0:T(8,128)(2,1)S(1)} collective-permute-done((bf16[128,1152]{1,0:T(8,128)(2,1)S(1)}, bf16[128,1152]{1,0:T(8,128)(2,1)S(1)}, u32[]{:S(2)}, u32[]{:S(2)}) %collective-permute-start.47) | collective-permute-done | bytes 294944 | tf_op jit(solution)/shard_map/ppermute | solution.py:34
  333.3 9.4 %collective-permute-done.109 = bf16[144,2592]{1,0:T(8,128)(2,1)S(1)} collective-permute-done((bf16[144,2592]{1,0:T(8,128)(2,1)S(1)}, bf16[144,2592]{1,0:T(8,128)(2,1)S(1)}, u32[]{:S(2)}, u32[]{:S(2)}) %collective-permute-start.109) | collective-permute-done | bytes 746528 | tf_op jit(solution)/shard_map/ppermute | solution.py:50
  342.7 8.7 %collective-permute-start.52 = (bf16[128,1152]{1,0:T(8,128)(2,1)}, bf16[128,1152]{1,0:T(8,128)(2,1)}, u32[]{:S(2)}, u32[]{:S(2)}) collective-permute-start(bf16[128,1152]{1,0:T(8,128)(2,1)} %subtract_convert_fusion), channel_id=1, source_target_pairs={{0,1},{1,0},{4,5},{5,4},{2,3},{3,2},{6,7},{7,6},{8,9},{9,8},{12,13... | collective-permute-start | bytes 884744 | tf_op jit(solution)/shard_map/ppermute | solution.py:38
  352.0 10.6 %collective-permute-done.97 = bf16[144,2592]{1,0:T(8,128)(2,1)} collective-permute-done((bf16[144,2592]{1,0:T(8,128)(2,1)}, bf16[144,2592]{1,0:T(8,128)(2,1)}, u32[]{:S(2)}, u32[]{:S(2)}) %collective-permute-start.97) | collective-permute-done | bytes 746528 | tf_op jit(solution)/shard_map/ppermute | solution.py:50
  372.7 5.1 collective-permute-done.98
  385.0 3.3 collective-permute-done.101
  394.4 3.5 collective-permute-start.114
  412.3 3.1 collective-permute-start.124
  416.3 2.9 fusion.41
  427.9 4.4 reshape.997
  432.3 3.5 copy.132
  435.8 3.1 copy.133
  441.2 3.9 gather_fusion.1
  445.1 3.5 fusion.163
  456.7 4.4 collective-permute-start.128
  461.9 3.0 copy.130
  510.0 2.8 fusion.164
  543.5 2.9 collective-permute-start.72
  547.6 3.1 collective-permute-done.106
  553.7 3.1 fusion.171
  561.1 2.7 collective-permute-start.75
  568.2 2.7 collective-permute-done.62
  579.2 3.6 collective-permute-done.79
  593.0 3.7 collective-permute-done.82
  606.7 3.8 fusion.172
  610.5 11.3 %multiply_reduce_fusion = (f32[576]{0:T(1024)S(1)}, f32[576,1728]{1,0:T(8,128)}, f32[576]{0:T(1024)S(1)}, f32[576,1728]{1,0:T(8,128)}) fusion(bf16[576,1728]{1,0:T(8,128)(2,1)S(1)} %copy-done.6, f32[576,864]{1,0:T(8,128)} %get-tuple-element.125, f32[576,864]{1,0:T(8,128)} %get-tuple-element.128, pred[]{:T(512)S(6)} %eq.135, ...), kind=kLoop, calls=%fused_computation.13 | loop fusion | flops 11942784 | bytes 19911168 | tf_op jit(solution)/shard_map/reduce_sum | solution.py:374
  621.8 21.4 %collective-permute-start.120 = (f32[2,576]{1,0:T(2,128)S(1)}, f32[2,576]{1,0:T(2,128)S(1)}, u32[]{:S(2)}, u32[]{:S(2)}) collective-permute-start(f32[2,576]{1,0:T(2,128)S(1)} %pad_maximum_fusion.23), channel_id=1, source_target_pairs={{0,1},{1,0},{4,5},{5,4},{2,3},{3,2},{6,7},{7,6},{8,9},{9,8},{12,13... | collective-permute-start | bytes 13832 | tf_op jit(solution)/shard_map/ppermute | solution.py:38
  646.2 5.6 fusion
  (705 shorter events, 310.0 us)
Async XLA Ops:
  7.2 146.1 %all-gather.3.cloned.1.call-start = ((), (), s32[]{:S(2)}) async-start(), calls=%async_computation | async-start | bytes 3655680 | tf_op jit(solution)/shard_map/all_gather | solution.py:233
  8.8 43.1 %collective-permute-start.11 = (bf16[1,576,128]{1,2,0:T(8,128)(2,1)}, bf16[1,576,128]{1,2,0:T(8,128)(2,1)}, u32[]{:S(2)}, u32[]{:S(2)}) collective-permute-start(bf16[1,576,128]{1,2,0:T(8,128)(2,1)} %maximum_bitcast_fusion), channel_id=1, source_target_pairs={{0,2},{1,3},{4,6},{5,7},{2,0},{3,1},{6,4},{7,5},{8,10},{9,11},{12,... | collective-permute-start | bytes 442376 | tf_op jit(solution)/shard_map/ppermute | solution.py:34
  13.3 39.3 %collective-permute-start.10 = (bf16[1,576,128]{1,2,0:T(8,128)(2,1)}, bf16[1,576,128]{1,2,0:T(8,128)(2,1)}, u32[]{:S(2)}, u32[]{:S(2)}) collective-permute-start(bf16[1,576,128]{1,2,0:T(8,128)(2,1)} %maximum_bitcast_fusion), channel_id=1, source_target_pairs={{0,1},{1,0},{4,5},{5,4},{2,3},{3,2},{6,7},{7,6},{8,9},{9,8},{12,13... | collective-permute-start | bytes 442376 | tf_op jit(solution)/shard_map/ppermute | solution.py:38
  14.2 49.6 %collective-permute-start.13 = (bf16[1,576,128]{1,2,0:T(8,128)(2,1)}, bf16[1,576,128]{1,2,0:T(8,128)(2,1)}, u32[]{:S(2)}, u32[]{:S(2)}) collective-permute-start(bf16[1,576,128]{1,2,0:T(8,128)(2,1)} %maximum_bitcast_fusion), channel_id=1, source_target_pairs={{0,4},{1,5},{4,2},{5,3},{2,6},{3,7},{6,0},{7,1},{8,12},{9,13},{12,... | collective-permute-start | bytes 442376 | tf_op jit(solution)/shard_map/ppermute | solution.py:34
  15.0 53.0 %collective-permute-start.15 = (bf16[1,576,128]{1,2,0:T(8,128)(2,1)}, bf16[1,576,128]{1,2,0:T(8,128)(2,1)}, u32[]{:S(2)}, u32[]{:S(2)}) collective-permute-start(bf16[1,576,128]{1,2,0:T(8,128)(2,1)} %maximum_bitcast_fusion), channel_id=1, source_target_pairs={{0,6},{1,7},{4,0},{5,1},{2,4},{3,5},{6,2},{7,3},{8,14},{9,15},{12,... | collective-permute-start | bytes 442376 | tf_op jit(solution)/shard_map/ppermute | solution.py:34
  19.7 24.8 %collective-permute-start.1 = (f32[4,576]{1,0:T(4,128)S(1)}, f32[4,576]{1,0:T(4,128)S(1)}, u32[]{:S(2)}, u32[]{:S(2)}) collective-permute-start(f32[4,576]{1,0:T(4,128)S(1)} %pad_maximum_fusion.22), channel_id=1, source_target_pairs={{0,4},{4,0},{1,5},{5,1},{2,6},{6,2},{3,7},{7,3},{8,12},{12,8},{9,1... | collective-permute-start | bytes 27656 | tf_op jit(solution)/shard_map/ppermute | solution.py:42
  49.7 44.5 %collective-permute-start.5 = (bf16[576,256]{1,0:T(8,128)(2,1)S(1)}, bf16[576,256]{1,0:T(8,128)(2,1)}, u32[]{:S(2)}, u32[]{:S(2)}) collective-permute-start(bf16[576,256]{1,0:T(8,128)(2,1)S(1)} %copy-done.22), channel_id=1, source_target_pairs={{0,4},{4,0},{1,5},{5,1},{2,6},{6,2},{3,7},{7,3},{8,12},{12,8},{9,1... | collective-permute-start | bytes 884744 | tf_op jit(solution)/shard_map/ppermute | solution.py:42
  61.4 17.1 %collective-permute-start.2 = (bf16[128,1152]{1,0:T(8,128)(2,1)}, bf16[128,1152]{1,0:T(8,128)(2,1)}, u32[]{:S(2)}, u32[]{:S(2)}) collective-permute-start(bf16[128,1152]{1,0:T(8,128)(2,1)} %get-tuple-element.121), channel_id=1, source_target_pairs={{0,1},{1,0},{4,5},{5,4},{2,3},{3,2},{6,7},{7,6},{8,9},{9,8},{12,13... | collective-permute-start | bytes 884744 | tf_op jit(solution)/shard_map/ppermute | solution.py:38
  63.8 14.9 %collective-permute-start.3 = (bf16[128,1152]{1,0:T(8,128)(2,1)}, bf16[128,1152]{1,0:T(8,128)(2,1)}, u32[]{:S(2)}, u32[]{:S(2)}) collective-permute-start(bf16[128,1152]{1,0:T(8,128)(2,1)} %get-tuple-element.121), channel_id=1, source_target_pairs={{0,2},{1,3},{4,6},{5,7},{2,0},{3,1},{6,4},{7,5},{8,10},{9,11},{12,... | collective-permute-start | bytes 884744 | tf_op jit(solution)/shard_map/ppermute | solution.py:34
  68.0 13.0 %collective-permute-start.6 = (bf16[128,1152]{1,0:T(8,128)(2,1)}, bf16[128,1152]{1,0:T(8,128)(2,1)}, u32[]{:S(2)}, u32[]{:S(2)}) collective-permute-start(bf16[128,1152]{1,0:T(8,128)(2,1)} %get-tuple-element.121), channel_id=1, source_target_pairs={{0,4},{1,5},{4,2},{5,3},{2,6},{3,7},{6,0},{7,1},{8,12},{9,13},{12,... | collective-permute-start | bytes 884744 | tf_op jit(solution)/shard_map/ppermute | solution.py:34
  78.6 23.8 %collective-permute-start.17 = (bf16[256,576]{0,1:T(8,128)(2,1)}, bf16[256,576]{0,1:T(8,128)(2,1)S(1)}, u32[]{:S(2)}, u32[]{:S(2)}) collective-permute-start(bf16[256,576]{0,1:T(8,128)(2,1)} %param.21), channel_id=1, source_target_pairs={{0,4},{4,0},{1,5},{5,1},{2,6},{6,2},{3,7},{7,3},{8,12},{12,8},{9,1... | collective-permute-start | bytes 884744 | tf_op jit(solution)/shard_map/ppermute | solution.py:42
  117.8 12.5 %collective-permute-start.22 = (bf16[128,1152]{1,0:T(8,128)(2,1)}, bf16[128,1152]{1,0:T(8,128)(2,1)S(1)}, u32[]{:S(2)}, u32[]{:S(2)}) collective-permute-start(bf16[128,1152]{1,0:T(8,128)(2,1)} %get-tuple-element.113), channel_id=1, source_target_pairs={{0,2},{1,3},{4,6},{5,7},{2,0},{3,1},{6,4},{7,5},{8,10},{9,11},{12,... | collective-permute-start | bytes 884744 | tf_op jit(solution)/shard_map/ppermute | solution.py:34
  121.0 14.0 %collective-permute-start.24 = (bf16[128,1152]{1,0:T(8,128)(2,1)}, bf16[128,1152]{1,0:T(8,128)(2,1)S(1)}, u32[]{:S(2)}, u32[]{:S(2)}) collective-permute-start(bf16[128,1152]{1,0:T(8,128)(2,1)} %get-tuple-element.113), channel_id=1, source_target_pairs={{0,4},{1,5},{4,2},{5,3},{2,6},{3,7},{6,0},{7,1},{8,12},{9,13},{12,... | collective-permute-start | bytes 884744 | tf_op jit(solution)/shard_map/ppermute | solution.py:34
  121.3 14.2 %collective-permute-start.26 = (bf16[128,1152]{1,0:T(8,128)(2,1)}, bf16[128,1152]{1,0:T(8,128)(2,1)S(1)}, u32[]{:S(2)}, u32[]{:S(2)}) collective-permute-start(bf16[128,1152]{1,0:T(8,128)(2,1)} %get-tuple-element.113), channel_id=1, source_target_pairs={{0,6},{1,7},{4,0},{5,1},{2,4},{3,5},{6,2},{7,3},{8,14},{9,15},{12,... | collective-permute-start | bytes 884744 | tf_op jit(solution)/shard_map/ppermute | solution.py:34
  123.7 24.3 %collective-permute-start.21 = (bf16[128,1152]{1,0:T(8,128)(2,1)}, bf16[128,1152]{1,0:T(8,128)(2,1)S(1)}, u32[]{:S(2)}, u32[]{:S(2)}) collective-permute-start(bf16[128,1152]{1,0:T(8,128)(2,1)} %get-tuple-element.113), channel_id=1, source_target_pairs={{0,1},{1,0},{4,5},{5,4},{2,3},{3,2},{6,7},{7,6},{8,9},{9,8},{12,13... | collective-permute-start | bytes 884744 | tf_op jit(solution)/shard_map/ppermute | solution.py:38
  130.3 19.1 %collective-permute-start.23 = (bf16[128,1152]{1,0:T(8,128)(2,1)S(1)}, bf16[128,1152]{1,0:T(8,128)(2,1)S(1)}, u32[]{:S(2)}, u32[]{:S(2)}) collective-permute-start(bf16[128,1152]{1,0:T(8,128)(2,1)S(1)} %collective-permute-done.22), channel_id=1, source_target_pairs={{0,1},{1,0},{4,5},{5,4},{2,3},{3,2},{6,7},{7,6},{8,9},{9,8},{12,13... | collective-permute-start | bytes 884744 | tf_op jit(solution)/shard_map/ppermute | solution.py:38
  135.0 16.0 %collective-permute-start.25 = (bf16[128,1152]{1,0:T(8,128)(2,1)S(1)}, bf16[128,1152]{1,0:T(8,128)(2,1)S(1)}, u32[]{:S(2)}, u32[]{:S(2)}) collective-permute-start(bf16[128,1152]{1,0:T(8,128)(2,1)S(1)} %collective-permute-done.24), channel_id=1, source_target_pairs={{0,1},{1,0},{4,5},{5,4},{2,3},{3,2},{6,7},{7,6},{8,9},{9,8},{12,13... | collective-permute-start | bytes 884744 | tf_op jit(solution)/shard_map/ppermute | solution.py:38
  135.5 17.0 %collective-permute-start.27 = (bf16[128,1152]{1,0:T(8,128)(2,1)S(1)}, bf16[128,1152]{1,0:T(8,128)(2,1)S(1)}, u32[]{:S(2)}, u32[]{:S(2)}) collective-permute-start(bf16[128,1152]{1,0:T(8,128)(2,1)S(1)} %collective-permute-done.26), channel_id=1, source_target_pairs={{0,1},{1,0},{4,5},{5,4},{2,3},{3,2},{6,7},{7,6},{8,9},{9,8},{12,13... | collective-permute-start | bytes 884744 | tf_op jit(solution)/shard_map/ppermute | solution.py:38
  203.9 22.4 %collective-permute-start.37 = (bf16[128,576]{1,0:T(8,128)(2,1)}, bf16[128,576]{1,0:T(8,128)(2,1)S(1)}, u32[]{:S(2)}, u32[]{:S(2)}) collective-permute-start(bf16[128,576]{1,0:T(8,128)(2,1)} %get-tuple-element.190), channel_id=1, source_target_pairs={{0,4},{4,0},{1,5},{5,1},{2,6},{6,2},{3,7},{7,3},{8,12},{12,8},{9,1... | collective-permute-start | bytes 442376 | tf_op jit(solution)/shard_map/ppermute | solution.py:42
  208.2 15.3 %collective-permute-start.33 = (bf16[128,1152]{1,0:T(8,128)(2,1)}, bf16[128,1152]{1,0:T(8,128)(2,1)S(1)}, u32[]{:S(2)}, u32[]{:S(2)}) collective-permute-start(bf16[128,1152]{1,0:T(8,128)(2,1)} %get-tuple-element.140), channel_id=1, source_target_pairs={{0,6},{1,7},{4,0},{5,1},{2,4},{3,5},{6,2},{7,3},{8,14},{9,15},{12,... | collective-permute-start | bytes 884744 | tf_op jit(solution)/shard_map/ppermute | solution.py:34
  210.9 13.8 %collective-permute-start.35 = (bf16[128,1152]{1,0:T(8,128)(2,1)S(1)}, bf16[128,1152]{1,0:T(8,128)(2,1)}, u32[]{:S(2)}, u32[]{:S(2)}) collective-permute-start(bf16[128,1152]{1,0:T(8,128)(2,1)S(1)} %get-tuple-element.139), channel_id=1, source_target_pairs={{0,2},{1,3},{4,6},{5,7},{2,0},{3,1},{6,4},{7,5},{8,10},{9,11},{12,... | collective-permute-start | bytes 884744 | tf_op jit(solution)/shard_map/ppermute | solution.py:34
  228.4 24.1 %collective-permute-start.38 = (bf16[128,1152]{1,0:T(8,128)(2,1)}, bf16[128,1152]{1,0:T(8,128)(2,1)}, u32[]{:S(2)}, u32[]{:S(2)}) collective-permute-start(bf16[128,1152]{1,0:T(8,128)(2,1)} %get-tuple-element.109), channel_id=1, source_target_pairs={{0,1},{1,0},{4,5},{5,4},{2,3},{3,2},{6,7},{7,6},{8,9},{9,8},{12,13... | collective-permute-start | bytes 884744 | tf_op jit(solution)/shard_map/ppermute | solution.py:38
  229.2 21.5 %collective-permute-start.39 = (bf16[128,1152]{1,0:T(8,128)(2,1)}, bf16[128,1152]{1,0:T(8,128)(2,1)}, u32[]{:S(2)}, u32[]{:S(2)}) collective-permute-start(bf16[128,1152]{1,0:T(8,128)(2,1)} %get-tuple-element.109), channel_id=1, source_target_pairs={{0,2},{1,3},{4,6},{5,7},{2,0},{3,1},{6,4},{7,5},{8,10},{9,11},{12,... | collective-permute-start | bytes 884744 | tf_op jit(solution)/shard_map/ppermute | solution.py:34
  229.8 21.7 %collective-permute-start.41 = (bf16[128,1152]{1,0:T(8,128)(2,1)}, bf16[128,1152]{1,0:T(8,128)(2,1)}, u32[]{:S(2)}, u32[]{:S(2)}) collective-permute-start(bf16[128,1152]{1,0:T(8,128)(2,1)} %get-tuple-element.109), channel_id=1, source_target_pairs={{0,4},{1,5},{4,2},{5,3},{2,6},{3,7},{6,0},{7,1},{8,12},{9,13},{12,... | collective-permute-start | bytes 884744 | tf_op jit(solution)/shard_map/ppermute | solution.py:34
  233.0 18.6 %collective-permute-start.43 = (bf16[128,1152]{1,0:T(8,128)(2,1)}, bf16[128,1152]{1,0:T(8,128)(2,1)S(1)}, u32[]{:S(2)}, u32[]{:S(2)}) collective-permute-start(bf16[128,1152]{1,0:T(8,128)(2,1)} %get-tuple-element.109), channel_id=1, source_target_pairs={{0,6},{1,7},{4,0},{5,1},{2,4},{3,5},{6,2},{7,3},{8,14},{9,15},{12,... | collective-permute-start | bytes 884744 | tf_op jit(solution)/shard_map/ppermute | solution.py:34
  233.3 16.7 %collective-permute-start.36 = (bf16[128,576]{0,1:T(8,128)(2,1)S(1)}, bf16[128,576]{0,1:T(8,128)(2,1)S(1)}, u32[]{:S(2)}, u32[]{:S(2)}) collective-permute-start(bf16[128,576]{0,1:T(8,128)(2,1)S(1)} %get-tuple-element.198), channel_id=1, source_target_pairs={{0,4},{4,0},{1,5},{5,1},{2,6},{6,2},{3,7},{7,3},{8,12},{12,8},{9,1... | collective-permute-start | bytes 442376 | tf_op jit(solution)/shard_map/ppermute | solution.py:42
  288.1 18.5 %collective-permute-start.46 = (bf16[128,1152]{1,0:T(8,128)(2,1)}, bf16[128,1152]{1,0:T(8,128)(2,1)S(1)}, u32[]{:S(2)}, u32[]{:S(2)}) collective-permute-start(bf16[128,1152]{1,0:T(8,128)(2,1)} %get-tuple-element.157), channel_id=1, source_target_pairs={{0,1},{1,0},{4,5},{5,4},{2,3},{3,2},{6,7},{7,6},{8,9},{9,8},{12,13... | collective-permute-start | bytes 884744 | tf_op jit(solution)/shard_map/ppermute | solution.py:38
  288.2 18.4 %collective-permute-start.48 = (bf16[128,1152]{1,0:T(8,128)(2,1)}, bf16[128,1152]{1,0:T(8,128)(2,1)S(1)}, u32[]{:S(2)}, u32[]{:S(2)}) collective-permute-start(bf16[128,1152]{1,0:T(8,128)(2,1)} %get-tuple-element.156), channel_id=1, source_target_pairs={{0,1},{1,0},{4,5},{5,4},{2,3},{3,2},{6,7},{7,6},{8,9},{9,8},{12,13... | collective-permute-start | bytes 884744 | tf_op jit(solution)/shard_map/ppermute | solution.py:38
  288.6 18.0 %collective-permute-start.50 = (bf16[128,1152]{1,0:T(8,128)(2,1)S(1)}, bf16[128,1152]{1,0:T(8,128)(2,1)}, u32[]{:S(2)}, u32[]{:S(2)}) collective-permute-start(bf16[128,1152]{1,0:T(8,128)(2,1)S(1)} %get-tuple-element.155), channel_id=1, source_target_pairs={{0,1},{1,0},{4,5},{5,4},{2,3},{3,2},{6,7},{7,6},{8,9},{9,8},{12,13... | collective-permute-start | bytes 884744 | tf_op jit(solution)/shard_map/ppermute | solution.py:38
  288.7 23.2 %collective-permute-start.45 = (bf16[128,1152]{1,0:T(8,128)(2,1)S(1)}, bf16[128,1152]{1,0:T(8,128)(2,1)S(1)}, u32[]{:S(2)}, u32[]{:S(2)}) collective-permute-start(bf16[128,1152]{1,0:T(8,128)(2,1)S(1)} %get-tuple-element.154), channel_id=1, source_target_pairs={{0,1},{1,0},{4,5},{5,4},{2,3},{3,2},{6,7},{7,6},{8,9},{9,8},{12,13... | collective-permute-start | bytes 884744 | tf_op jit(solution)/shard_map/ppermute | solution.py:38
  305.2 26.1 %collective-permute-start.107 = (bf16[144,2592]{1,0:T(8,128)(2,1)S(1)}, bf16[144,2592]{1,0:T(8,128)(2,1)S(1)}, u32[]{:S(2)}, u32[]{:S(2)}) collective-permute-start(bf16[144,2592]{1,0:T(8,128)(2,1)S(1)} %get-tuple-element.141), channel_id=1, source_target_pairs={{0,8},{8,16},{16,24},{24,0},{32,40},{40,48},{48,56},{56,32},{64,72... | collective-permute-start | bytes 2239496 | tf_op jit(solution)/shard_map/ppermute | solution.py:50
  307.7 15.8 %collective-permute-start.47 = (bf16[128,1152]{1,0:T(8,128)(2,1)S(1)}, bf16[128,1152]{1,0:T(8,128)(2,1)S(1)}, u32[]{:S(2)}, u32[]{:S(2)}) collective-permute-start(bf16[128,1152]{1,0:T(8,128)(2,1)S(1)} %get-tuple-element.135), channel_id=1, source_target_pairs={{0,4},{1,5},{4,2},{5,3},{2,6},{3,7},{6,0},{7,1},{8,12},{9,13},{12,... | collective-permute-start | bytes 884744 | tf_op jit(solution)/shard_map/ppermute | solution.py:34
  307.8 18.4 %collective-permute-start.49 = (bf16[128,1152]{1,0:T(8,128)(2,1)S(1)}, bf16[128,1152]{1,0:T(8,128)(2,1)S(1)}, u32[]{:S(2)}, u32[]{:S(2)}) collective-permute-start(bf16[128,1152]{1,0:T(8,128)(2,1)S(1)} %get-tuple-element.137), channel_id=1, source_target_pairs={{0,6},{1,7},{4,0},{5,1},{2,4},{3,5},{6,2},{7,3},{8,14},{9,15},{12,... | collective-permute-start | bytes 884744 | tf_op jit(solution)/shard_map/ppermute | solution.py:34
  310.5 16.9 %collective-permute-start.51 = (bf16[128,1152]{1,0:T(8,128)(2,1)S(1)}, bf16[128,1152]{1,0:T(8,128)(2,1)S(1)}, u32[]{:S(2)}, u32[]{:S(2)}) collective-permute-start(bf16[128,1152]{1,0:T(8,128)(2,1)S(1)} %get-tuple-element.136), channel_id=1, source_target_pairs={{0,2},{1,3},{4,6},{5,7},{2,0},{3,1},{6,4},{7,5},{8,10},{9,11},{12,... | collective-permute-start | bytes 884744 | tf_op jit(solution)/shard_map/ppermute | solution.py:34
  312.0 20.9 %collective-permute-start.108 = (bf16[144,2592]{1,0:T(8,128)(2,1)S(1)}, bf16[144,2592]{1,0:T(8,128)(2,1)S(1)}, u32[]{:S(2)}, u32[]{:S(2)}) collective-permute-start(bf16[144,2592]{1,0:T(8,128)(2,1)S(1)} %get-tuple-element.143), channel_id=1, source_target_pairs={{0,24},{8,0},{16,8},{24,16},{32,56},{40,32},{48,40},{56,48},{64,88... | collective-permute-start | bytes 2239496 | tf_op jit(solution)/shard_map/ppermute | solution.py:50
  323.6 19.1 %collective-permute-start.109 = (bf16[144,2592]{1,0:T(8,128)(2,1)S(1)}, bf16[144,2592]{1,0:T(8,128)(2,1)S(1)}, u32[]{:S(2)}, u32[]{:S(2)}) collective-permute-start(bf16[144,2592]{1,0:T(8,128)(2,1)S(1)} %get-tuple-element.142), channel_id=1, source_target_pairs={{0,16},{8,24},{16,0},{24,8},{32,48},{40,56},{48,32},{56,40},{64,80... | collective-permute-start | bytes 2239496 | tf_op jit(solution)/shard_map/ppermute | solution.py:50
  326.2 25.8 %collective-permute-start.95 = (bf16[144,2592]{1,0:T(8,128)(2,1)}, bf16[144,2592]{1,0:T(8,128)(2,1)}, u32[]{:S(2)}, u32[]{:S(2)}) collective-permute-start(bf16[144,2592]{1,0:T(8,128)(2,1)} %get-tuple-element.144), channel_id=1, source_target_pairs={{0,32},{8,40},{16,48},{24,56},{32,64},{40,72},{48,80},{56,88},{64,... | collective-permute-start | bytes 2239496 | tf_op jit(solution)/shard_map/ppermute | solution.py:50
  327.4 24.6 %collective-permute-start.96 = (bf16[144,2592]{1,0:T(8,128)(2,1)}, bf16[144,2592]{1,0:T(8,128)(2,1)}, u32[]{:S(2)}, u32[]{:S(2)}) collective-permute-start(bf16[144,2592]{1,0:T(8,128)(2,1)} %get-tuple-element.146), channel_id=1, source_target_pairs={{0,96},{8,104},{16,112},{24,120},{32,0},{40,8},{48,16},{56,24},{64... | collective-permute-start | bytes 2239496 | tf_op jit(solution)/shard_map/ppermute | solution.py:50
  331.3 31.3 %collective-permute-start.97 = (bf16[144,2592]{1,0:T(8,128)(2,1)}, bf16[144,2592]{1,0:T(8,128)(2,1)}, u32[]{:S(2)}, u32[]{:S(2)}) collective-permute-start(bf16[144,2592]{1,0:T(8,128)(2,1)} %get-tuple-element.145), channel_id=1, source_target_pairs={{0,64},{8,72},{16,80},{24,88},{32,96},{40,104},{48,112},{56,120},{... | collective-permute-start | bytes 2239496 | tf_op jit(solution)/shard_map/ppermute | solution.py:50
  332.8 35.4 %collective-permute-start.53 = (bf16[128,1152]{1,0:T(8,128)(2,1)}, bf16[128,1152]{1,0:T(8,128)(2,1)}, u32[]{:S(2)}, u32[]{:S(2)}) collective-permute-start(bf16[128,1152]{1,0:T(8,128)(2,1)} %subtract_convert_fusion), channel_id=1, source_target_pairs={{0,2},{1,3},{4,6},{5,7},{2,0},{3,1},{6,4},{7,5},{8,10},{9,11},{12,... | collective-permute-start | bytes 884744 | tf_op jit(solution)/shard_map/ppermute | solution.py:34
  342.7 58.3 %collective-permute-start.52 = (bf16[128,1152]{1,0:T(8,128)(2,1)}, bf16[128,1152]{1,0:T(8,128)(2,1)}, u32[]{:S(2)}, u32[]{:S(2)}) collective-permute-start(bf16[128,1152]{1,0:T(8,128)(2,1)} %subtract_convert_fusion), channel_id=1, source_target_pairs={{0,1},{1,0},{4,5},{5,4},{2,3},{3,2},{6,7},{7,6},{8,9},{9,8},{12,13... | collective-permute-start | bytes 884744 | tf_op jit(solution)/shard_map/ppermute | solution.py:38
  365.5 12.2 %collective-permute-start.98 = (bf16[36,2592]{1,0:T(8,128)(2,1)S(1)}, bf16[36,2592]{1,0:T(8,128)(2,1)S(1)}, u32[]{:S(2)}, u32[]{:S(2)}) collective-permute-start(bf16[36,2592]{1,0:T(8,128)(2,1)S(1)} %get-tuple-element.181), channel_id=1, source_target_pairs={{0,8},{8,16},{16,24},{24,0},{32,40},{40,48},{48,56},{56,32},{64,72... | collective-permute-start | bytes 559880 | tf_op jit(solution)/shard_map/ppermute | solution.py:50
  378.3 22.7 %collective-permute-start.54 = (bf16[128,1152]{1,0:T(8,128)(2,1)}, bf16[128,1152]{1,0:T(8,128)(2,1)}, u32[]{:S(2)}, u32[]{:S(2)}) collective-permute-start(bf16[128,1152]{1,0:T(8,128)(2,1)} %collective-permute-done.53), channel_id=1, source_target_pairs={{0,1},{1,0},{4,5},{5,4},{2,3},{3,2},{6,7},{7,6},{8,9},{9,8},{12,13... | collective-permute-start | bytes 884744 | tf_op jit(solution)/shard_map/ppermute | solution.py:38
  394.4 79.2 %collective-permute-start.114 = (bf16[36,2592]{1,0:T(8,128)(2,1)}, bf16[36,2592]{1,0:T(8,128)(2,1)}, u32[]{:S(2)}, u32[]{:S(2)}) collective-permute-start(bf16[36,2592]{1,0:T(8,128)(2,1)} %collective-permute-done.113), channel_id=1, source_target_pairs={{0,32},{8,40},{16,48},{24,56},{32,64},{40,72},{48,80},{56,88},{64,... | collective-permute-start | bytes 559880 | tf_op jit(solution)/shard_map/ppermute | solution.py:50
  397.9 77.7 %collective-permute-start.115 = (bf16[36,2592]{1,0:T(8,128)(2,1)}, bf16[36,2592]{1,0:T(8,128)(2,1)}, u32[]{:S(2)}, u32[]{:S(2)}) collective-permute-start(bf16[36,2592]{1,0:T(8,128)(2,1)} %collective-permute-done.113), channel_id=1, source_target_pairs={{0,96},{8,104},{16,112},{24,120},{32,0},{40,8},{48,16},{56,24},{64... | collective-permute-start | bytes 559880 | tf_op jit(solution)/shard_map/ppermute | solution.py:50
  409.9 42.3 %collective-permute-start.122 = (f32[22,128]{1,0:T(8,128)S(1)}, f32[22,128]{1,0:T(8,128)S(1)}, u32[]{:S(2)}, u32[]{:S(2)}) collective-permute-start(f32[22,128]{1,0:T(8,128)S(1)} %maximum_bitcast_fusion.1), channel_id=1, source_target_pairs={{0,64},{8,72},{16,80},{24,88},{32,96},{40,104},{48,112},{56,120},{... | collective-permute-start | bytes 33800 | tf_op jit(solution)/shard_map/ppermute | solution.py:50
  412.3 39.9 %collective-permute-start.123 = (f32[22,128]{1,0:T(8,128)S(1)}, f32[22,128]{1,0:T(8,128)S(1)}, u32[]{:S(2)}, u32[]{:S(2)}) collective-permute-start(f32[22,128]{1,0:T(8,128)S(1)} %maximum_bitcast_fusion.1), channel_id=1, source_target_pairs={{0,32},{8,40},{16,48},{24,56},{32,64},{40,72},{48,80},{56,88},{64,... | collective-permute-start | bytes 33800 | tf_op jit(solution)/shard_map/ppermute | solution.py:50
  412.3 39.9 %collective-permute-start.124 = (f32[22,128]{1,0:T(8,128)S(1)}, f32[22,128]{1,0:T(8,128)S(1)}, u32[]{:S(2)}, u32[]{:S(2)}) collective-permute-start(f32[22,128]{1,0:T(8,128)S(1)} %maximum_bitcast_fusion.1), channel_id=1, source_target_pairs={{0,96},{8,104},{16,112},{24,120},{32,0},{40,8},{48,16},{56,24},{64... | collective-permute-start | bytes 33800 | tf_op jit(solution)/shard_map/ppermute | solution.py:50
  483.0 19.8 %collective-permute-start.55 = (bf16[128,1152]{1,0:T(8,128)(2,1)}, bf16[128,1152]{1,0:T(8,128)(2,1)}, u32[]{:S(2)}, u32[]{:S(2)}) collective-permute-start(bf16[128,1152]{1,0:T(8,128)(2,1)} %get-tuple-element.150), channel_id=1, source_target_pairs={{0,1},{1,0},{4,5},{5,4},{2,3},{3,2},{6,7},{7,6},{8,9},{9,8},{12,13... | collective-permute-start | bytes 884744 | tf_op jit(solution)/shard_map/ppermute | solution.py:38
  487.8 13.0 %collective-permute-start.70 = (bf16[576,128]{1,0:T(8,128)(2,1)}, bf16[576,128]{1,0:T(8,128)(2,1)}, u32[]{:S(2)}, u32[]{:S(2)}) collective-permute-start(bf16[576,128]{1,0:T(8,128)(2,1)} %get-tuple-element.149), channel_id=1, source_target_pairs={{0,2},{1,3},{4,6},{5,7},{2,0},{3,1},{6,4},{7,5},{8,10},{9,11},{12,... | collective-permute-start | bytes 442376 | tf_op jit(solution)/shard_map/ppermute | solution.py:34
  490.9 14.5 %collective-permute-start.57 = (bf16[128,1152]{1,0:T(8,128)(2,1)}, bf16[128,1152]{1,0:T(8,128)(2,1)}, u32[]{:S(2)}, u32[]{:S(2)}) collective-permute-start(bf16[128,1152]{1,0:T(8,128)(2,1)} %get-tuple-element.132), channel_id=1, source_target_pairs={{0,4},{1,5},{4,2},{5,3},{2,6},{3,7},{6,0},{7,1},{8,12},{9,13},{12,... | collective-permute-start | bytes 884744 | tf_op jit(solution)/shard_map/ppermute | solution.py:34
  491.3 16.8 %collective-permute-start.59 = (bf16[128,1152]{1,0:T(8,128)(2,1)}, bf16[128,1152]{1,0:T(8,128)(2,1)}, u32[]{:S(2)}, u32[]{:S(2)}) collective-permute-start(bf16[128,1152]{1,0:T(8,128)(2,1)} %get-tuple-element.134), channel_id=1, source_target_pairs={{0,6},{1,7},{4,0},{5,1},{2,4},{3,5},{6,2},{7,3},{8,14},{9,15},{12,... | collective-permute-start | bytes 884744 | tf_op jit(solution)/shard_map/ppermute | solution.py:34
  494.4 13.7 %collective-permute-start.61 = (bf16[128,1152]{1,0:T(8,128)(2,1)}, bf16[128,1152]{1,0:T(8,128)(2,1)}, u32[]{:S(2)}, u32[]{:S(2)}) collective-permute-start(bf16[128,1152]{1,0:T(8,128)(2,1)} %get-tuple-element.133), channel_id=1, source_target_pairs={{0,2},{1,3},{4,6},{5,7},{2,0},{3,1},{6,4},{7,5},{8,10},{9,11},{12,... | collective-permute-start | bytes 884744 | tf_op jit(solution)/shard_map/ppermute | solution.py:34
  500.8 40.8 %collective-permute-start.104 = (bf16[144,2592]{1,0:T(8,128)(2,1)}, bf16[144,2592]{1,0:T(8,128)(2,1)}, u32[]{:S(2)}, u32[]{:S(2)}) collective-permute-start(bf16[144,2592]{1,0:T(8,128)(2,1)} %reshape.1008), channel_id=1, source_target_pairs={{0,32},{8,40},{16,48},{24,56},{32,64},{40,72},{48,80},{56,88},{64,... | collective-permute-start | bytes 2239496 | tf_op jit(solution)/shard_map/ppermute | solution.py:50
  502.8 40.7 %collective-permute-start.105 = (bf16[144,2592]{1,0:T(8,128)(2,1)}, bf16[144,2592]{1,0:T(8,128)(2,1)}, u32[]{:S(2)}, u32[]{:S(2)}) collective-permute-start(bf16[144,2592]{1,0:T(8,128)(2,1)} %reshape.1008), channel_id=1, source_target_pairs={{0,96},{8,104},{16,112},{24,120},{32,0},{40,8},{48,16},{56,24},{64... | collective-permute-start | bytes 2239496 | tf_op jit(solution)/shard_map/ppermute | solution.py:50
  505.4 14.2 %collective-permute-start.63 = (bf16[576,512]{1,0:T(8,128)(2,1)}, bf16[576,512]{1,0:T(8,128)(2,1)}, u32[]{:S(2)}, u32[]{:S(2)}) collective-permute-start(bf16[576,512]{1,0:T(8,128)(2,1)} %fusion.54), channel_id=1, source_target_pairs={{0,4},{4,0},{1,5},{5,1},{2,6},{6,2},{3,7},{7,3},{8,12},{12,8},{9,1... | collective-permute-start | bytes 1769480 | tf_op jit(solution)/shard_map/ppermute | solution.py:42
  535.9 14.8 %collective-permute-start.106 = (bf16[144,2592]{1,0:T(8,128)(2,1)}, bf16[144,2592]{1,0:T(8,128)(2,1)S(1)}, u32[]{:S(2)}, u32[]{:S(2)}) collective-permute-start(bf16[144,2592]{1,0:T(8,128)(2,1)} %reshape.1008), channel_id=1, source_target_pairs={{0,64},{8,72},{16,80},{24,88},{32,96},{40,104},{48,112},{56,120},{... | collective-permute-start | bytes 2239496 | tf_op jit(solution)/shard_map/ppermute | solution.py:50
  536.3 61.8 %collective-permute-start.117 = (bf16[144,2592]{1,0:T(8,128)(2,1)}, bf16[144,2592]{1,0:T(8,128)(2,1)}, u32[]{:S(2)}, u32[]{:S(2)}) collective-permute-start(bf16[144,2592]{1,0:T(8,128)(2,1)} %reshape.1011), channel_id=1, source_target_pairs={{0,8},{8,16},{16,24},{24,0},{32,40},{40,48},{48,56},{56,32},{64,72... | collective-permute-start | bytes 2239496 | tf_op jit(solution)/shard_map/ppermute | solution.py:50
  538.8 61.4 %collective-permute-start.118 = (bf16[144,2592]{1,0:T(8,128)(2,1)}, bf16[144,2592]{1,0:T(8,128)(2,1)}, u32[]{:S(2)}, u32[]{:S(2)}) collective-permute-start(bf16[144,2592]{1,0:T(8,128)(2,1)} %reshape.1011), channel_id=1, source_target_pairs={{0,24},{8,0},{16,8},{24,16},{32,56},{40,32},{48,40},{56,48},{64,88... | collective-permute-start | bytes 2239496 | tf_op jit(solution)/shard_map/ppermute | solution.py:50
  542.2 14.6 %collective-permute-start.71 = (bf16[144,384]{1,0:T(8,128)(2,1)S(1)}, bf16[144,384]{1,0:T(8,128)(2,1)S(1)}, u32[]{:S(2)}, u32[]{:S(2)}) collective-permute-start(bf16[144,384]{1,0:T(8,128)(2,1)S(1)} %get-tuple-element.187), channel_id=1, source_target_pairs={{0,8},{8,16},{16,24},{24,0},{32,40},{40,48},{48,56},{56,32},{64,72... | collective-permute-start | bytes 331784 | tf_op jit(solution)/shard_map/ppermute | solution.py:50
  543.5 13.3 %collective-permute-start.72 = (bf16[144,384]{1,0:T(8,128)(2,1)S(1)}, bf16[144,384]{1,0:T(8,128)(2,1)S(1)}, u32[]{:S(2)}, u32[]{:S(2)}) collective-permute-start(bf16[144,384]{1,0:T(8,128)(2,1)S(1)} %get-tuple-element.189), channel_id=1, source_target_pairs={{0,24},{8,0},{16,8},{24,16},{32,56},{40,32},{48,40},{56,48},{64,88... | collective-permute-start | bytes 331784 | tf_op jit(solution)/shard_map/ppermute | solution.py:50
  565.7 36.6 %collective-permute-start.119 = (bf16[144,2592]{1,0:T(8,128)(2,1)}, bf16[144,2592]{1,0:T(8,128)(2,1)}, u32[]{:S(2)}, u32[]{:S(2)}) collective-permute-start(bf16[144,2592]{1,0:T(8,128)(2,1)} %reshape.1011), channel_id=1, source_target_pairs={{0,16},{8,24},{16,0},{24,8},{32,48},{40,56},{48,32},{56,40},{64,80... | collective-permute-start | bytes 2239496 | tf_op jit(solution)/shard_map/ppermute | solution.py:50
  568.1 15.9 %collective-permute-start.92 = (bf16[144,256]{1,0:T(8,128)(2,1)}, bf16[144,256]{1,0:T(8,128)(2,1)}, u32[]{:S(2)}, u32[]{:S(2)}) collective-permute-start(bf16[144,256]{1,0:T(8,128)(2,1)} %reshape.1004), channel_id=1, source_target_pairs={{0,32},{8,40},{16,48},{24,56},{32,64},{40,72},{48,80},{56,88},{64,... | collective-permute-start | bytes 221192 | tf_op jit(solution)/shard_map/ppermute | solution.py:50
  621.8 24.0 %collective-permute-start.120 = (f32[2,576]{1,0:T(2,128)S(1)}, f32[2,576]{1,0:T(2,128)S(1)}, u32[]{:S(2)}, u32[]{:S(2)}) collective-permute-start(f32[2,576]{1,0:T(2,128)S(1)} %pad_maximum_fusion.23), channel_id=1, source_target_pairs={{0,1},{1,0},{4,5},{5,4},{2,3},{3,2},{6,7},{7,6},{8,9},{9,8},{12,13... | collective-permute-start | bytes 13832 | tf_op jit(solution)/shard_map/ppermute | solution.py:38
  (179 other events, 1159.2 us)
Sparse Core Ops, SparseCore 0:
  63.9 47.8 all-gather.2
